TPU v7x, 32 devices: a whole 2x2x4 slice. The times are simulated.
32 devices in a mesh: seq: 4 (over y, x), dp: 8 (over z, core).
Axes of the slice: x: 2, y: 2, z: 4, core: 2. Of those that a mesh axis runs over, the one named last changes fastest.
Arguments:
- codes: int32 [16, 3072], P('dp', 'seq'), may hold values from 0 to 511
- actions: int32 [16, 3072], P('dp', 'seq'), may hold values from 0 to 17
- next_codes: int32 [16, 3072], P('dp', 'seq'), may hold values from 0 to 511
- lengths: int32 [16, 8], P('dp'), may hold values from 0 to 3072, as said below
- rewards: float32 [16, 3072], P('dp', 'seq'), may hold values from -6 to 6
- continues: float32 [16, 3072], P('dp', 'seq'), may hold values from 0 to 1
- target_values: float32 [16, 3072], P('dp', 'seq'), may hold values from -6 to 6
- table: float32 [530, 256], replicated, may hold values from -6 to 6
- table_m: float32 [530, 256], replicated, may hold values from -1.1444092e-05 to 1.1444092e-05
- table_v: float32 [530, 256], replicated, may hold values from 5.41632e-14 to 2.166528e-13
- attn_in: float32 [2, 256, 768], replicated, may hold values from -0.375 to 0.375
- attn_in_m: float32 [2, 256, 768], replicated, may hold values from -6.1035156e-05 to 6.1035156e-05
- attn_in_v: float32 [2, 256, 768], replicated, may hold values from 1.35408e-12 to 5.41632e-12
- attn_out: float32 [2, 256, 256], replicated, may hold values from -1 to 1
- attn_out_m: float32 [2, 256, 256], replicated, may hold values from -6.1035156e-05 to 6.1035156e-05
- attn_out_v: float32 [2, 256, 256], replicated, may hold values from 1.35408e-12 to 5.41632e-12
- ffn_in: float32 [2, 256, 1024], replicated, may hold values from -0.375 to 0.375
- ffn_in_m: float32 [2, 256, 1024], replicated, may hold values from -6.1035156e-05 to 6.1035156e-05
- ffn_in_v: float32 [2, 256, 1024], replicated, may hold values from 1.35408e-12 to 5.41632e-12
- ffn_out: float32 [2, 1024, 256], replicated, may hold values from -0.1875 to 0.1875
- ffn_out_m: float32 [2, 1024, 256], replicated, may hold values from -6.1035156e-05 to 6.1035156e-05
- ffn_out_v: float32 [2, 1024, 256], replicated, may hold values from 1.35408e-12 to 5.41632e-12
- gains: float32 [5, 256], replicated, may hold values from 0.5 to 1.5
- gains_m: float32 [5, 256], replicated, may hold values from -6.1035156e-05 to 6.1035156e-05
- gains_v: float32 [5, 256], replicated, may hold values from 1.35408e-12 to 5.41632e-12
- readout: float32 [256, 533], replicated, may hold values from -0.375 to 0.375
- readout_m: float32 [256, 533], replicated, may hold values from -6.1035156e-05 to 6.1035156e-05
- readout_v: float32 [256, 533], replicated, may hold values from 1.35408e-12 to 5.41632e-12
Outputs:
- table_new: float32 [530, 256], replicated
- table_m_new: float32 [530, 256], replicated
- table_v_new: float32 [530, 256], replicated
- attn_in_new: float32 [2, 256, 768], replicated
- attn_in_m_new: float32 [2, 256, 768], replicated
- attn_in_v_new: float32 [2, 256, 768], replicated
- attn_out_new: float32 [2, 256, 256], replicated
- attn_out_m_new: float32 [2, 256, 256], replicated
- attn_out_v_new: float32 [2, 256, 256], replicated
- ffn_in_new: float32 [2, 256, 1024], replicated
- ffn_in_m_new: float32 [2, 256, 1024], replicated
- ffn_in_v_new: float32 [2, 256, 1024], replicated
- ffn_out_new: float32 [2, 1024, 256], replicated
- ffn_out_m_new: float32 [2, 1024, 256], replicated
- ffn_out_v_new: float32 [2, 1024, 256], replicated
- gains_new: float32 [5, 256], replicated
- gains_m_new: float32 [5, 256], replicated
- gains_v_new: float32 [5, 256], replicated
- readout_new: float32 [256, 533], replicated
- readout_m_new: float32 [256, 533], replicated
- readout_v_new: float32 [256, 533], replicated
- loss_sum: float32 [], replicated
- step_count: float32 [], replicated
- grad_norm: float32 [], replicated
Inputs may be any that keep to these rules, and one draw needn't show every extreme that they name: Each sequence's lengths sum to 3072; lengths may be 0; in each block of 2 sequences one sequence is a single episode.
All inputs are finite; a program needn't handle non-finite values.
Results may differ from a plain program's by a relative error of at most 0.0066.
Values may be sent and summed in bfloat16 or wider, within the bound.
A program may use at most 256 MiB of HBM per device.

v0:
```python
import math

import jax
import jax.numpy as jnp
from jax import lax
from jax.sharding import PartitionSpec as P

HEADS = 8
VOCAB = 512
SEG = 48
STEP = 5


EPS_NORM = 1e-06
BETA_ONE = 0.9
BETA_TWO = 0.999
RATES = (0.25, 0.02, 0.08, 0.02, 0.02, 0.25, 0.02)
DECAY = 0.01
ADAM_EPS = 1e-08
CLIP_NORM = 0.05
GAMMA = 0.985
LAMBDA_RET = 0.95
ENTROPY_COEF = 0.05


def from_behind(value, axis, steps):
    count = lax.axis_size(axis)
    leading, last = (max(0, -steps), min(count, count - steps))
    return lax.ppermute(value, axis, [(source, source + steps) for source in range(leading, last)])


def matmul_f(left, right):
    return jnp.dot(left, right, preferred_element_type=jnp.float32)


def matmul_left(left, right):
    return lax.dot_general(
        left, right, (((0,), (0,)), ((), ())), preferred_element_type=jnp.float32
    )


def matmul_right(left, right):
    return lax.dot_general(
        left, right, (((1,), (1,)), ((), ())), preferred_element_type=jnp.float32
    )


def rms_forward(hidden, gain_vec):
    inv_rms = lax.rsqrt(jnp.mean(hidden * hidden, axis=-1, keepdims=True) + EPS_NORM)
    return (hidden * inv_rms * gain_vec, inv_rms)


def rms_backward(grad_in, hidden, inv_rms, gain_vec):
    weighted = grad_in * gain_vec
    grad_hidden = inv_rms * weighted - hidden * inv_rms * inv_rms * inv_rms * jnp.mean(
        weighted * hidden, axis=-1, keepdims=True
    )
    return (grad_hidden, jnp.sum(grad_in * hidden * inv_rms, axis=0))


def gelu_tanh(values):
    return jax.nn.gelu(values, approximate=True)


def episode_marks(lengths, positions):
    ep_ends = jnp.cumsum(lengths, axis=-1)
    passed = positions[None, :, None] >= ep_ends[:, None, :]
    doc_ids = jnp.sum(passed.astype(jnp.int32), axis=-1)
    doc_ids = jnp.where(positions[None, :] < 0, jnp.int32(-1), doc_ids)
    ep_start = jnp.max(jnp.where(passed, ep_ends[:, None, :], 0), axis=-1)
    ep_final = jnp.any(positions[None, :, None] + 1 == ep_ends[:, None, :], axis=-1)
    return (doc_ids, positions[None, :] - ep_start, ep_final)


def tile_allowed(doc_ids, span_len):
    batch_rows = doc_ids.shape[0]
    tiles = span_len // SEG
    key_docs = jnp.concatenate(
        [
            doc_ids[:, :span_len].reshape(batch_rows, tiles, SEG),
            doc_ids[:, SEG:].reshape(batch_rows, tiles, SEG),
        ],
        axis=-1,
    )
    query_docs = doc_ids[:, SEG:].reshape(batch_rows, tiles, SEG)
    causal = jnp.arange(2 * SEG)[None, :] <= SEG + jnp.arange(SEG)[:, None]
    return causal[None, None] & (key_docs[:, :, None, :] == query_docs[..., None])


def position_code(rel_pos, dims):
    frequency = jnp.exp(
        jnp.arange(dims // 2).astype(jnp.float32) * (-2.0 * math.log(10000.0) / dims)
    )
    angles = rel_pos[..., None].astype(jnp.float32) * frequency
    return jnp.concatenate([jnp.sin(angles), jnp.cos(angles)], axis=-1)


def lambda_returns(rewards, continues, values):
    rew_steps = jnp.moveaxis(rewards, -1, 0)
    cont_steps = jnp.moveaxis(continues, -1, 0)
    value_steps = jnp.moveaxis(values, -1, 0)

    def back_step(later_ret, step_items):
        reward_now, cont_now, value_next = step_items
        now_ret = reward_now + GAMMA * cont_now * (
            (1.0 - LAMBDA_RET) * value_next + LAMBDA_RET * later_ret
        )
        return (now_ret, now_ret)

    last_ret = value_steps[-1]
    unused, early_ret = lax.scan(
        back_step, last_ret, (rew_steps[:-1], cont_steps[:-1], value_steps[1:]), reverse=True
    )
    full_ret = jnp.concatenate([early_ret, last_ret[None]], axis=0)
    return jnp.moveaxis(full_ret, 0, -1)


def token_losses(outputs, next_codes, actions, rewards, continues, target_values, returns):
    logits = outputs[..., :VOCAB]
    picked = jnp.take_along_axis(logits, next_codes[..., None], axis=-1)[..., 0]
    cross_ent = jax.nn.logsumexp(logits, axis=-1) - picked
    reward_err = 0.5 * jnp.square(outputs[..., VOCAB] - rewards)
    end_logit = outputs[..., VOCAB + 1]
    ending = jax.nn.softplus(end_logit) - continues * end_logit
    critic = outputs[..., VOCAB + 2]
    log_policy = jax.nn.log_softmax(outputs[..., VOCAB + 3 :], axis=-1)
    chosen = jnp.take_along_axis(log_policy, actions[..., None], axis=-1)[..., 0]
    entropy = -jnp.sum(jnp.exp(log_policy) * log_policy, axis=-1)
    policy = -(returns - target_values) * chosen - ENTROPY_COEF * entropy
    value_err = 0.5 * jnp.square(critic - returns)
    return cross_ent + reward_err + ending + policy + value_err


def adam_update(weight, first_mom, second_mom, clipped, rate):
    new_first = BETA_ONE * first_mom + (1.0 - BETA_ONE) * clipped
    new_second = BETA_TWO * second_mom + (1.0 - BETA_TWO) * clipped * clipped
    ratio = (
        new_first
        / (1.0 - BETA_ONE**STEP)
        / (jnp.sqrt(new_second / (1.0 - BETA_TWO**STEP)) + ADAM_EPS)
    )
    return (weight - rate * (ratio + DECAY * weight), new_first, new_second)


def layer_forward(hidden, w_in, w_out, w_up, w_down, gain_attn, gain_ffn, allowed):
    tok_rows, dims = hidden.shape
    batch_size, tiles = (allowed.shape[0], allowed.shape[1])
    head_count = HEADS
    normed, inv_attn = rms_forward(hidden, gain_attn)
    h_in = normed.astype(jnp.bfloat16)
    mixed = matmul_f(h_in, w_in.astype(jnp.bfloat16)).astype(jnp.bfloat16)
    query_part, key_part, value_part = jnp.split(mixed, 3, axis=1)
    own_keys = key_part.reshape(batch_size, tiles, SEG, dims)
    own_values = value_part.reshape(batch_size, tiles, SEG, dims)
    last_kv = jnp.stack([own_keys[:, -1], own_values[:, -1]])
    memory_kv = from_behind(last_kv, "seq", 1)
    prev_keys = jnp.concatenate([memory_kv[0][:, None], own_keys[:, :-1]], axis=1)
    prev_values = jnp.concatenate([memory_kv[1][:, None], own_values[:, :-1]], axis=1)
    key_heads = jnp.concatenate([prev_keys, own_keys], axis=2).reshape(
        batch_size, tiles, 2 * SEG, head_count, -1
    )
    value_heads = jnp.concatenate([prev_values, own_values], axis=2).reshape(
        batch_size, tiles, 2 * SEG, head_count, -1
    )
    query_heads = query_part.reshape(batch_size, tiles, SEG, head_count, -1)
    score_scale = query_heads.shape[-1] ** (-0.5)
    scores = (
        jnp.einsum("btqhe,btkhe->bthqk", query_heads, key_heads, preferred_element_type=jnp.float32)
        * score_scale
    )
    attn_probs = jax.nn.softmax(jnp.where(allowed[:, :, None], scores, -1000000000.0), axis=-1)
    attn_mix = (
        jnp.einsum(
            "bthqk,btkhe->btqhe",
            attn_probs.astype(jnp.bfloat16),
            value_heads,
            preferred_element_type=jnp.float32,
        )
        .reshape(tok_rows, dims)
        .astype(jnp.bfloat16)
    )
    hidden_mid = hidden + matmul_f(attn_mix, w_out.astype(jnp.bfloat16))
    normed_mid, inv_ffn = rms_forward(hidden_mid, gain_ffn)
    h_mid = normed_mid.astype(jnp.bfloat16)
    up_proj = matmul_f(h_mid, w_up.astype(jnp.bfloat16))
    act_out = gelu_tanh(up_proj).astype(jnp.bfloat16)
    hidden_out = hidden_mid + matmul_f(act_out, w_down.astype(jnp.bfloat16))
    kept_vals = (
        hidden,
        inv_attn,
        h_in,
        query_heads,
        key_heads,
        value_heads,
        attn_probs,
        attn_mix,
        hidden_mid,
        inv_ffn,
        h_mid,
        up_proj,
        act_out,
    )
    return (hidden_out, kept_vals)


def layer_backward(grad_out, kept_vals, w_in, w_out, w_up, w_down, gain_attn, gain_ffn):
    (
        hidden,
        inv_attn,
        h_in,
        query_heads,
        key_heads,
        value_heads,
        attn_probs,
        attn_mix,
        hidden_mid,
        inv_ffn,
        h_mid,
        up_proj,
        act_out,
    ) = kept_vals
    tok_rows, dims = hidden.shape
    score_scale = query_heads.shape[-1] ** (-0.5)
    grad_low = grad_out.astype(jnp.bfloat16)
    grad_down = matmul_left(act_out, grad_low)
    grad_act = matmul_right(grad_low, w_down.astype(jnp.bfloat16))
    unused, gelu_pull = jax.vjp(gelu_tanh, up_proj)
    grad_upproj = gelu_pull(grad_act)[0].astype(jnp.bfloat16)
    grad_up = matmul_left(h_mid, grad_upproj)
    grad_hmid = matmul_right(grad_upproj, w_up.astype(jnp.bfloat16))
    grad_ffn_in, grad_gain_ffn = rms_backward(grad_hmid, hidden_mid, inv_ffn, gain_ffn)
    grad_mid = grad_out + grad_ffn_in
    mid_low = grad_mid.astype(jnp.bfloat16)
    grad_wout = matmul_left(attn_mix, mid_low)
    grad_mix = (
        matmul_right(mid_low, w_out.astype(jnp.bfloat16))
        .astype(jnp.bfloat16)
        .reshape(query_heads.shape)
    )
    grad_probs = jnp.einsum(
        "btqhe,btkhe->bthqk", grad_mix, value_heads, preferred_element_type=jnp.float32
    )
    grad_values = jnp.einsum(
        "bthqk,btqhe->btkhe",
        attn_probs.astype(jnp.bfloat16),
        grad_mix,
        preferred_element_type=jnp.float32,
    )
    grad_scores = (
        attn_probs * (grad_probs - jnp.sum(grad_probs * attn_probs, axis=-1, keepdims=True))
    ).astype(jnp.bfloat16)
    grad_query = (
        jnp.einsum("bthqk,btkhe->btqhe", grad_scores, key_heads, preferred_element_type=jnp.float32)
        * score_scale
    )
    grad_keys = (
        jnp.einsum(
            "bthqk,btqhe->btkhe", grad_scores, query_heads, preferred_element_type=jnp.float32
        )
        * score_scale
    )
    back_kv = jnp.stack([grad_keys[:, 0, :SEG], grad_values[:, 0, :SEG]])
    returned = from_behind(back_kv.astype(jnp.bfloat16), "seq", -1).astype(back_kv.dtype)
    later_keys = jnp.concatenate([grad_keys[:, 1:, :SEG], returned[0][:, None]], axis=1)
    later_values = jnp.concatenate([grad_values[:, 1:, :SEG], returned[1][:, None]], axis=1)
    grad_key = (grad_keys[:, :, SEG:] + later_keys).reshape(tok_rows, dims)
    grad_value = (grad_values[:, :, SEG:] + later_values).reshape(tok_rows, dims)
    grad_mixed = jnp.concatenate(
        [grad_query.reshape(tok_rows, dims), grad_key, grad_value], axis=1
    ).astype(jnp.bfloat16)
    grad_win = matmul_left(h_in, grad_mixed)
    grad_hin = matmul_right(grad_mixed, w_in.astype(jnp.bfloat16))
    grad_attn_in, grad_gain_attn = rms_backward(grad_hin, hidden, inv_attn, gain_attn)
    return (
        grad_mid + grad_attn_in,
        (grad_win, grad_wout, grad_up, grad_down, grad_gain_attn, grad_gain_ffn),
    )


def local(
    codes,
    actions,
    next_codes,
    lengths,
    rewards,
    continues,
    target_values,
    table,
    table_m,
    table_v,
    attn_in,
    attn_in_m,
    attn_in_v,
    attn_out,
    attn_out_m,
    attn_out_v,
    ffn_in,
    ffn_in_m,
    ffn_in_v,
    ffn_out,
    ffn_out_m,
    ffn_out_v,
    gains,
    gains_m,
    gains_v,
    readout,
    readout_m,
    readout_v,
):
    batch_size, dev_len = codes.shape
    tok_rows = batch_size * dev_len
    tiles = dev_len // SEG
    dims = table.shape[1]
    layers = attn_in.shape[0]
    seq_index = lax.axis_index("seq")
    positions = seq_index * dev_len - SEG + jnp.arange(dev_len + SEG)
    doc_ids, rel_pos, ep_final = episode_marks(lengths, positions)
    allowed = tile_allowed(doc_ids, dev_len)
    is_valid = jnp.logical_not(ep_final[:, SEG:]).astype(jnp.float32).reshape(tok_rows)
    returns = lambda_returns(
        rewards.reshape(batch_size, tiles, SEG),
        continues.reshape(batch_size, tiles, SEG),
        target_values.reshape(batch_size, tiles, SEG),
    ).reshape(batch_size, dev_len)
    span = jnp.arange(table.shape[0])
    onehot = (
        ((span == codes[..., None]) | (span == actions[..., None] + VOCAB))
        .astype(jnp.bfloat16)
        .reshape(tok_rows, -1)
    )
    hidden = matmul_f(onehot, table.astype(jnp.bfloat16)) + position_code(
        rel_pos[:, SEG:], dims
    ).reshape(tok_rows, dims)
    saved = []
    for layer_idx in range(layers):
        hidden, kept_vals = layer_forward(
            hidden,
            attn_in[layer_idx],
            attn_out[layer_idx],
            ffn_in[layer_idx],
            ffn_out[layer_idx],
            gains[2 * layer_idx],
            gains[2 * layer_idx + 1],
            allowed,
        )
        saved.append(kept_vals)
    final_normed, final_inv = rms_forward(hidden, gains[2 * layers])
    final_in = final_normed.astype(jnp.bfloat16)
    outputs = matmul_f(final_in, readout.astype(jnp.bfloat16))

    def loss_of(head_out):
        return jnp.sum(
            is_valid
            * token_losses(
                head_out,
                next_codes.reshape(tok_rows),
                actions.reshape(tok_rows),
                rewards.reshape(tok_rows),
                continues.reshape(tok_rows),
                target_values.reshape(tok_rows),
                returns.reshape(tok_rows),
            )
        )

    loss_val, loss_pull = jax.vjp(loss_of, outputs)
    grad_outputs = loss_pull(jnp.ones((), jnp.float32))[0].astype(jnp.bfloat16)
    grad_readout = matmul_left(final_in, grad_outputs)
    grad_final = matmul_right(grad_outputs, readout.astype(jnp.bfloat16))
    grad_hidden, grad_gain_final = rms_backward(grad_final, hidden, final_inv, gains[2 * layers])
    layer_grads = [None] * layers
    for layer_idx in reversed(range(layers)):
        grad_hidden, layer_grads[layer_idx] = layer_backward(
            grad_hidden,
            saved[layer_idx],
            attn_in[layer_idx],
            attn_out[layer_idx],
            ffn_in[layer_idx],
            ffn_out[layer_idx],
            gains[2 * layer_idx],
            gains[2 * layer_idx + 1],
        )
    grad_table = matmul_left(onehot, grad_hidden.astype(jnp.bfloat16))
    grad_win = jnp.stack([entry[0] for entry in layer_grads])
    grad_wout = jnp.stack([entry[1] for entry in layer_grads])
    grad_up = jnp.stack([entry[2] for entry in layer_grads])
    grad_down = jnp.stack([entry[3] for entry in layer_grads])
    gain_rows = []
    for entry in layer_grads:
        gain_rows.append(entry[4])
        gain_rows.append(entry[5])
    gain_rows.append(grad_gain_final)
    grad_gains = jnp.stack(gain_rows)
    partial_value = (
        lax.psum(grad_table.astype(jnp.bfloat16), "seq").astype(jnp.float32),
        lax.psum(grad_win.astype(jnp.bfloat16), "seq").astype(jnp.float32),
        lax.psum(grad_wout.astype(jnp.bfloat16), "seq").astype(jnp.float32),
        lax.psum(grad_up.astype(jnp.bfloat16), "seq").astype(jnp.float32),
        lax.psum(grad_down.astype(jnp.bfloat16), "seq").astype(jnp.float32),
        lax.psum(grad_gains.astype(jnp.bfloat16), "seq").astype(jnp.float32),
        lax.psum(grad_readout.astype(jnp.bfloat16), "seq").astype(jnp.float32),
        lax.psum(loss_val.astype(jnp.bfloat16), "seq").astype(jnp.float32),
        lax.psum(jnp.sum(is_valid).astype(jnp.bfloat16), "seq").astype(jnp.float32),
    )
    params = (table, attn_in, attn_out, ffn_in, ffn_out, gains, readout)
    firsts = (table_m, attn_in_m, attn_out_m, ffn_in_m, ffn_out_m, gains_m, readout_m)
    seconds = (table_v, attn_in_v, attn_out_v, ffn_in_v, ffn_out_v, gains_v, readout_v)
    results = []
    summed = lax.psum(
        (
            partial_value[0],
            partial_value[1],
            partial_value[2],
            partial_value[3],
            partial_value[4],
            partial_value[5],
            partial_value[6],
            partial_value[7],
            partial_value[8],
        ),
        "dp",
    )
    loss_sum = summed[7]
    step_count = summed[8]
    averaged = [grad / step_count for grad in summed[:7]]
    grad_norm = jnp.sqrt(sum((jnp.sum(grad * grad) for grad in averaged)))
    factor = jnp.minimum(1.0, CLIP_NORM / grad_norm)
    for slot in range(7):
        results.extend(
            adam_update(
                params[slot], firsts[slot], seconds[slot], averaged[slot] * factor, RATES[slot]
            )
        )
    return tuple(results) + (loss_sum, step_count, grad_norm)


def solution(mesh):
    return jax.shard_map(
        local,
        mesh=mesh,
        in_specs=(
            P("dp", "seq"),
            P("dp", "seq"),
            P("dp", "seq"),
            P("dp", None),
            P("dp", "seq"),
            P("dp", "seq"),
            P("dp", "seq"),
            P(),
            P(),
            P(),
            P(),
            P(),
            P(),
            P(),
            P(),
            P(),
            P(),
            P(),
            P(),
            P(),
            P(),
            P(),
            P(),
            P(),
            P(),
            P(),
            P(),
            P(),
        ),
        out_specs=(
            P(),
            P(),
            P(),
            P(),
            P(),
            P(),
            P(),
            P(),
            P(),
            P(),
            P(),
            P(),
            P(),
            P(),
            P(),
            P(),
            P(),
            P(),
            P(),
            P(),
            P(),
            P(),
            P(),
            P(),
        ),
        check_vma=False,
    )
```

profile of v0, /device:TPU:0, one launch (start us, length us, event | category | flops | bytes accessed | tf_op | source)
XLA Modules:
  0.0 680.8 jit_solution(7754385365695565637)
XLA Ops:
  20.1 5.7 collective-permute-start
  54.4 4.7 copy.273
  59.1 4.7 copy.267
  63.8 4.7 copy.272
  73.0 9.4 %fusion.172 = (f32[2,16,8,48]{3,2,1,0:T(8,128)}, f32[2,16,8,48,96]{4,3,2,1,0:T(8,128)}) fusion(pred[2,16,48,96]{3,2,1,0:T(8,128)(4,1)} %compare_and_fusion, bf16[2,16,48,8,32]{2,4,3,1,0:T(8,128)(2,1)} %copy.273, bf16[2,16,48,8,32]{2,4,3,1,0:T(8,128)(2,1)} %copy.272, bf16[2,15,48,8,32]{2,4,3,1,0:T(8,128)(2,1)S(1)} %bitcast.242, ...), kind=kOutput, calls=%fused_computation.368 | convolution fusion | flops 84934752 | bytes 7274496 | tf_op jit(solution)/shard_map/sub | solution.py:171
  82.5 5.3 fusion.154
  92.3 4.6 convert_element_type.228
  129.5 4.7 copy.285
  134.1 4.7 copy.279
  138.8 4.7 copy.284
  148.1 9.4 %fusion.173 = (f32[2,16,8,48]{3,2,1,0:T(8,128)}, f32[2,16,8,48,96]{4,3,2,1,0:T(8,128)}) fusion(pred[2,16,48,96]{3,2,1,0:T(8,128)(4,1)} %compare_and_fusion, bf16[2,16,48,8,32]{2,4,3,1,0:T(8,128)(2,1)} %copy.285, bf16[2,16,48,8,32]{2,4,3,1,0:T(8,128)(2,1)} %copy.284, bf16[2,15,48,8,32]{2,4,3,1,0:T(8,128)(2,1)S(1)} %bitcast.246, ...), kind=kOutput, calls=%fused_computation.369 | convolution fusion | flops 84934752 | bytes 7274496 | tf_op jit(solution)/shard_map/sub | solution.py:171
  157.4 4.9 fusion.155
  166.9 4.8 convert_element_type.241
  191.0 5.5 fusion.23
  209.2 4.8 fusion.48
  214.0 10.6 %multiply_reduce_fusion.1 = (f32[2,16,8,48]{3,2,1,0:T(8,128)S(1)}, f32[2,16,8,48,96]{4,3,2,1,0:T(8,128)}) fusion(f32[2,16,8,48,96]{4,3,2,1,0:T(8,128)} %get-tuple-element.295, f32[2,16,8,48]{3,2,1,0:T(8,128)S(1)} %copy-done.83, bf16[2,16,48,8,32]{2,4,3,1,0:T(8,128)(2,1)S(1)} %copy-done.27, bf16[2,15,48,8,32]{2,4,3,1,0:T(8,128)(2,1)} %bitcast.248, ...), kind=kOutput, calls=%fused_computation.37 | convolution fusion | flops 83742720 | bytes 11894784 | tf_op jit(solution)/shard_map/btqhe,btkhe->bthqk/dot_general | solution.py:240
  224.7 7.4 %multiply_convert_fusion.1 = bf16[2,16,8,48,96]{4,3,2,1,0:T(8,128)(2,1)S(1)} fusion(f32[2,16,8,48,96]{4,3,2,1,0:T(8,128)} %get-tuple-element.303, f32[2,16,8,48]{3,2,1,0:T(8,128)S(1)} %get-tuple-element.302, f32[2,16,8,48,96]{4,3,2,1,0:T(8,128)S(1)} %bitcast.239, f32[2,16,8,48]{3,2,1,0:T(8,128)S(1)} %copy-done.83), kind=kLoop, calls=%fused_computation.36 | loop fusion | flops 4718592 | bytes 11894784 | tf_op jit(solution)/shard_map/convert_element_type | solution.py:251
  239.8 5.2 reshape.575
  260.3 5.4 reshape.576
  265.7 4.6 fusion.28
  273.0 5.2 reshape.577
  291.4 5.4 fusion.16
  315.1 9.0 %multiply_reduce_fusion = (f32[2,16,8,48]{3,2,1,0:T(8,128)S(1)}, f32[2,16,8,48,96]{4,3,2,1,0:T(8,128)S(1)}) fusion(f32[2,16,8,48,96]{4,3,2,1,0:T(8,128)} %get-tuple-element.289, f32[2,16,8,48]{3,2,1,0:T(8,128)S(1)} %copy-done.81, bf16[2,16,48,8,32]{2,4,3,1,0:T(8,128)(2,1)S(1)} %copy-done.23, bf16[2,15,48,8,32]{2,4,3,1,0:T(8,128)(2,1)} %bitcast.244, ...), kind=kOutput, calls=%fused_computation.35 | convolution fusion | flops 83742720 | bytes 11894784 | tf_op jit(solution)/shard_map/btqhe,btkhe->bthqk/dot_general | solution.py:240
  357.2 4.7 reshape.580
  361.9 4.6 fusion.26
  369.2 5.2 reshape.581
  382.8 12.7 %gather_fusion.1 = f32[1536]{0:T(1024)S(1)} fusion(f32[1536,18]{0,1:T(8,128)S(1)} %copy-done.1, s32[1536]{0:T(1024)S(1)} %get-tuple-element.312), kind=kCustom, calls=%fused_computation.1 | custom fusion | bytes 24576 | tf_op jit(solution)/shard_map/jvp(jit(take_along_axis))/gather | solution.py:127
  395.6 12.7 %gather_fusion = f32[1536]{0:T(1024)S(1)} fusion(f32[1536,512]{0,1:T(8,128)S(1)} %copy-done.2, s32[1536]{0:T(1024)S(1)} %get-tuple-element.311), kind=kCustom, calls=%fused_computation | custom fusion | bytes 24576 | tf_op jit(solution)/shard_map/jvp(jit(take_along_axis))/gather | solution.py:120
  409.2 11.0 %all-reduce.6 = (bf16[]{:T(256)}, bf16[5,256]{1,0:T(8,128)(2,1)S(1)}, bf16[]{:T(256)}) all-reduce(bf16[]{:T(256)} %get-tuple-element.189, bf16[5,256]{1,0:T(8,128)(2,1)S(1)} %stack.107, bf16[]{:T(256)} %get-tuple-element.188), channel_id=1, replica_groups=mesh['seq'=4,'dp'=8] {'seq'}, use_global_device_ids=true, to_apply=%region_30.31 | all-reduce | flops 1282 | bytes 5128 | tf_op jit(solution)/shard_map/psum | solution.py:402
  420.3 60.7 %all-reduce.11.cloned.1.call-done = (bf16[530,256]{1,0:T(8,128)(2,1)}, bf16[2,256,768]{2,1,0:T(8,128)(2,1)}, bf16[2,256,256]{2,1,0:T(8,128)(2,1)}, bf16[2,256,10...) async-done(((bf16[530,256]{1,0:T(8,128)(2,1)}, bf16[2,256,768]{2,1,0:T(8,128)(2,1)}, bf16[2,256,256]{2,1,0:T(8,128)(2,1)}, ...) | async-done | bytes 3690000 | tf_op jit(solution)/shard_map/psum | solution.py:394
  480.9 150.4 %all-reduce.12 = (f32[530,256]{1,0:T(8,128)}, f32[]{:T(128)}, f32[2,256,768]{2,1,0:T(8,128)}, f32[2,256,256]{2,1,0:T(8,128)S(1)}, f32[2,256,1024]{2,1,0:T(8,128)...) all-reduce(bf16[530,256]{1,0:T(8,128)(2,1)} %get-tuple-element.214,, ...), channel_id=1, replica_groups=mesh['seq'=4,'dp'=8] {'dp'}, use_global_device_ids=true, to_apply=%region_28.29 | all-reduce | flops 1846274 | bytes 11077644 | tf_op jit(solution)/shard_map/psum | solution.py:408
  663.4 4.5 multiply_subtract_fusion
  (579 shorter events, 257.7 us)
Async XLA Ops:
  7.2 473.7 %all-reduce.11.cloned.1.call-start = ((), (), s32[]{:S(2)}) async-start(), calls=%async_computation | async-start | bytes 7389184 | tf_op jit(solution)/shard_map/psum | solution.py:394
  8.8 89.1 %copy-start.133 = (f32[1,256]{1,0:T(1,128)}, f32[1,256]{1,0:T(1,128)S(1)}, u32[]{:S(2)}) copy-start(f32[1,256]{1,0:T(1,128)S(1)} %get-tuple-element.278) | copy-start | bytes 3076
  17.3 79.6 %copy-start.12 = (f32[1536,256]{0,1:T(8,128)}, f32[1536,256]{0,1:T(8,128)S(1)}, u32[]{:S(2)}) copy-start(f32[1536,256]{0,1:T(8,128)S(1)} %get-tuple-element.287) | copy-start | bytes 4718596
  18.4 10.0 %copy-start.107 = (f32[2,768]{1,0:T(2,128)S(1)}, f32[2,768]{1,0:T(2,128)}, u32[]{:S(2)}) copy-start(f32[2,768]{1,0:T(2,128)} %param.34) | copy-start | bytes 18436
  18.4 10.0 %copy-start.110 = (f32[2,768]{1,0:T(2,128)S(1)}, f32[2,768]{1,0:T(2,128)}, u32[]{:S(2)}) copy-start(f32[2,768]{1,0:T(2,128)} %param.35) | copy-start | bytes 18436
  20.1 48.4 %collective-permute-start = (bf16[2,2,48,256]{3,2,1,0:T(8,128)(2,1)}, bf16[2,2,48,256]{3,2,1,0:T(8,128)(2,1)}, u32[]{:S(2)}, u32[]{:S(2)}) collective-permute-start(bf16[2,2,48,256]{3,2,1,0:T(8,128)(2,1)} %pad_maximum_fusion.10), channel_id=1, source_target_pairs={{0,8},{8,16},{16,24},{1,9},{9,17},{17,25},{2,10},{10,18},{18,26},{... | collective-permute-start | bytes 294920 | tf_op jit(solution)/shard_map/ppermute | solution.py:29
  26.9 10.7 %copy-start.124 = (pred[2,816]{1,0:T(4,128)(4,1)}, pred[2,816]{1,0:T(4,128)(4,1)S(1)}, u32[]{:S(2)}) copy-start(pred[2,816]{1,0:T(4,128)(4,1)S(1)} %compare_reduce_fusion) | copy-start | bytes 4900
  47.0 26.1 %copy-start.34 = (bf16[2,15,48,256]{2,3,1,0:T(8,128)(2,1)}, bf16[2,15,48,256]{2,3,1,0:T(8,128)(2,1)S(1)}, u32[]{:S(2)}) copy-start(bf16[2,15,48,256]{2,3,1,0:T(8,128)(2,1)S(1)} %copy.270) | copy-start | bytes 2211844
  105.1 38.4 %collective-permute-start.1 = (bf16[2,2,48,256]{3,2,1,0:T(8,128)(2,1)}, bf16[2,2,48,256]{3,2,1,0:T(8,128)(2,1)}, u32[]{:S(2)}, u32[]{:S(2)}) collective-permute-start(bf16[2,2,48,256]{3,2,1,0:T(8,128)(2,1)} %pad_maximum_fusion.11), channel_id=1, source_target_pairs={{0,8},{8,16},{16,24},{1,9},{9,17},{17,25},{2,10},{10,18},{18,26},{... | collective-permute-start | bytes 294920 | tf_op jit(solution)/shard_map/ppermute | solution.py:29
  122.0 26.1 %copy-start.37 = (bf16[2,15,48,256]{2,3,1,0:T(8,128)(2,1)}, bf16[2,15,48,256]{2,3,1,0:T(8,128)(2,1)S(1)}, u32[]{:S(2)}) copy-start(bf16[2,15,48,256]{2,3,1,0:T(8,128)(2,1)S(1)} %copy.282) | copy-start | bytes 2211844
  209.2 15.5 %slice-start.2 = ((s8[6291456]{0:T(1024)(128)(4,1)}), s8[4194304]{0:T(1024)(128)(4,1)S(1)}, s32[]{:S(2)}) async-start(s8[6291456]{0:T(1024)(128)(4,1)} %bitcast.238), calls=%async_computation.3 | async-start | bytes 8388608
  214.0 23.1 %copy-start.4 = (f32[2,16,96,8,32]{2,4,3,0,1:T(8,128)}, f32[2,16,96,8,32]{2,4,3,0,1:T(8,128)S(1)}, u32[]{:S(2)}) copy-start(f32[2,16,96,8,32]{2,4,3,0,1:T(8,128)S(1)} %fusion.48) | copy-start | bytes 9437188
  214.0 10.6 %slice-start.3 = ((s8[6291456]{0:T(1024)(128)(4,1)}), s8[2097152]{0:T(1024)(128)(4,1)S(1)}, s32[]{:S(2)}) async-start(s8[6291456]{0:T(1024)(128)(4,1)} %bitcast.238), calls=%async_computation.4 | async-start | bytes 4194304
  246.0 10.4 %collective-permute-start.2 = (bf16[2,2,48,8,32]{2,4,3,1,0:T(8,128)(2,1)S(1)}, bf16[2,2,48,8,32]{2,4,3,1,0:T(8,128)(2,1)S(1)}, u32[]{:S(2)}, u32[]{:S(2)}) collective-permute-start(bf16[2,2,48,8,32]{2,4,3,1,0:T(8,128)(2,1)S(1)} %pad_maximum_fusion.7), channel_id=1, source_target_pairs={{8,0},{16,8},{24,16},{9,1},{17,9},{25,17},{10,2},{18,10},{26,18},{... | collective-permute-start | bytes 294920 | tf_op jit(solution)/shard_map/ppermute | solution.py:29
  311.2 13.0 %slice-start = ((s8[6291456]{0:T(1024)(128)(4,1)}), s8[4194304]{0:T(1024)(128)(4,1)S(1)}, s32[]{:S(2)}) async-start(s8[6291456]{0:T(1024)(128)(4,1)} %bitcast.236), calls=%async_computation.1 | async-start | bytes 8388608
  315.1 19.2 %copy-start.3 = (f32[2,16,96,8,32]{2,4,3,0,1:T(8,128)}, f32[2,16,96,8,32]{2,4,3,0,1:T(8,128)S(1)}, u32[]{:S(2)}) copy-start(f32[2,16,96,8,32]{2,4,3,0,1:T(8,128)S(1)} %fusion.51) | copy-start | bytes 9437188
  342.4 10.1 %collective-permute-start.3 = (bf16[2,2,48,8,32]{2,4,3,1,0:T(8,128)(2,1)S(1)}, bf16[2,2,48,8,32]{2,4,3,1,0:T(8,128)(2,1)S(1)}, u32[]{:S(2)}, u32[]{:S(2)}) collective-permute-start(bf16[2,2,48,8,32]{2,4,3,1,0:T(8,128)(2,1)S(1)} %pad_maximum_fusion.8), channel_id=1, source_target_pairs={{8,0},{16,8},{24,16},{9,1},{17,9},{25,17},{10,2},{18,10},{26,18},{... | collective-permute-start | bytes 294920 | tf_op jit(solution)/shard_map/ppermute | solution.py:29
  382.7 12.8 %copy-start.120 = (f32[1536]{0:T(1024)S(1)}, f32[1536]{0:T(1024)}, u32[]{:S(2)}) copy-start(f32[1536]{0:T(1024)} %get-tuple-element.184) | copy-start | bytes 18436
  382.7 12.8 %copy-start.2 = (f32[1536,512]{0,1:T(8,128)S(1)}, f32[1536,512]{0,1:T(8,128)}, u32[]{:S(2)}) copy-start(f32[1536,512]{0,1:T(8,128)} %get-tuple-element.247) | copy-start | bytes 9437188
  395.5 12.8 %copy-start.144 = (bf16[256]{0:T(256)(128)(2,1)S(1)}, bf16[256]{0:T(256)(128)(2,1)}, u32[]{:S(2)}) copy-start(bf16[256]{0:T(256)(128)(2,1)} %get-tuple-element.174) | copy-start | bytes 1540
  395.6 12.9 %copy-start.145 = (bf16[256]{0:T(256)(128)(2,1)S(1)}, bf16[256]{0:T(256)(128)(2,1)}, u32[]{:S(2)}) copy-start(bf16[256]{0:T(256)(128)(2,1)} %get-tuple-element.176) | copy-start | bytes 1540
  395.6 12.9 %copy-start.106 = (f32[2,768]{1,0:T(2,128)S(1)}, f32[2,768]{1,0:T(2,128)}, u32[]{:S(2)}) copy-start(f32[2,768]{1,0:T(2,128)} %param.36) | copy-start | bytes 18436
  395.6 12.9 %copy-start.109 = (f32[2,768]{1,0:T(2,128)S(1)}, f32[2,768]{1,0:T(2,128)}, u32[]{:S(2)}) copy-start(f32[2,768]{1,0:T(2,128)} %param.34) | copy-start | bytes 18436
  395.6 12.9 %copy-start.112 = (f32[2,768]{1,0:T(2,128)S(1)}, f32[2,768]{1,0:T(2,128)}, u32[]{:S(2)}) copy-start(f32[2,768]{1,0:T(2,128)} %param.35) | copy-start | bytes 18436
  395.6 12.9 %copy-start.125 = (pred[2,816]{1,0:T(4,128)(4,1)S(1)}, pred[2,816]{1,0:T(4,128)(4,1)}, u32[]{:S(2)}) copy-start(pred[2,816]{1,0:T(4,128)(4,1)} %copy-done.124) | copy-start | bytes 4900
  395.6 13.5 %copy-start.143 = (bf16[256]{0:T(256)(128)(2,1)S(1)}, bf16[256]{0:T(256)(128)(2,1)}, u32[]{:S(2)}) copy-start(bf16[256]{0:T(256)(128)(2,1)} %get-tuple-element.178) | copy-start | bytes 1540
  395.6 13.5 %copy-start.146 = (bf16[256]{0:T(256)(128)(2,1)S(1)}, bf16[256]{0:T(256)(128)(2,1)}, u32[]{:S(2)}) copy-start(bf16[256]{0:T(256)(128)(2,1)} %get-tuple-element.180) | copy-start | bytes 1540
  637.5 11.0 %copy-start.132 = (f32[5,256]{1,0:T(8,128)S(1)}, f32[5,256]{1,0:T(8,128)}, u32[]{:S(2)}) copy-start(f32[5,256]{1,0:T(8,128)} %param.52) | copy-start | bytes 15364
  637.5 11.0 %copy-start.137 = (f32[5,256]{1,0:T(8,128)S(1)}, f32[5,256]{1,0:T(8,128)}, u32[]{:S(2)}) copy-start(f32[5,256]{1,0:T(8,128)} %param.53) | copy-start | bytes 15364
  637.5 11.0 %copy-start.138 = (f32[5,256]{1,0:T(8,128)S(1)}, f32[5,256]{1,0:T(8,128)}, u32[]{:S(2)}) copy-start(f32[5,256]{1,0:T(8,128)} %param.54) | copy-start | bytes 15364
  637.5 12.5 %copy-start.54 = (f32[2,256,256]{2,1,0:T(8,128)S(1)}, f32[2,256,256]{2,1,0:T(8,128)}, u32[]{:S(2)}) copy-start(f32[2,256,256]{2,1,0:T(8,128)} %param.43) | copy-start | bytes 1572868
  642.4 11.1 %copy-start.60 = (f32[256,533]{0,1:T(8,128)S(1)}, f32[256,533]{0,1:T(8,128)}, u32[]{:S(2)}) copy-start(f32[256,533]{0,1:T(8,128)} %param.55) | copy-start | bytes 1637380
  (126 other events, 486.0 us)
Sparse Core Ops, SparseCore 0:
  381.8 99.0 all-reduce.10
where the time goes:
time: 688 us; the launch traced here: 681 us
  local copies, waits for them, and re-layouts  207 us (30%)
  blocking collectives  161 us (23%)
  matrix products  115 us (17%)
  other arithmetic  99.3 us (14%)
  waiting for transfers between devices  62.9 us (9%)
  between operations  22.3 us (3%)
  starting transfers between devices  12.1 us (2%)
    psum x1, blocking collectives, local(): lax.psum((partial_value[0], partial_value[1], partial_value[2], partial_v...  150 us
    psum x1, waiting for transfers between devices, local(): lax.psum(grad_table.astype(jnp.bfloat16), 'seq').astype(jnp.float32)  60.7 us
    dot_general x9, matrix products, matmul_right(): lax.dot_general(left, right, (((1,), (1,)), ((), ())), preferred_element_...  23 us
    sub x7, other arithmetic, adam_update(): return (weight - rate * (ratio + DECAY * weight), new_first, new_second)  22.4 us
    dot_general x10, matrix products, matmul_left(): lax.dot_general(left, right, (((0,), (0,)), ((), ())), preferred_element_...  21.5 us
    dot_general x2, matrix products, layer_backward(): jnp.einsum('btqhe,btkhe->bthqk', grad_mix, value_heads, preferred_element...  19.6 us
    sub x2, matrix products, layer_forward(): jax.nn.softmax(jnp.where(allowed[:, :, None], scores, -1000000000.0), axi...  18.8 us
    reshape x4, local copies, waits for them, and re-layouts, layer_forward(): query_heads = query_part.reshape(batch_size, tiles, SEG, head_count, -1)  18.3 us
  transfers between devices with their start and end apart: 5, of which 2 were waited for; matrix products, arithmetic and copies ran while one was open for 17% of the time, Pallas kernels for 0%

commit v1 on v0

v1 whole, which is shorter than its diff:
```python
import functools
import math

import jax
import jax.numpy as jnp
from jax import lax
from jax.experimental import pallas as pl
from jax.experimental.pallas import tpu as pltpu
from jax.sharding import PartitionSpec as P

HEADS = 8
VOCAB = 512
SEG = 48
STEP = 5

EPS_NORM = 1e-06
BETA_ONE = 0.9
BETA_TWO = 0.999
RATES = (0.25, 0.02, 0.08, 0.02, 0.02, 0.25, 0.02)
DECAY = 0.01
ADAM_EPS = 1e-08
CLIP_NORM = 0.05
GAMMA = 0.985
LAMBDA_RET = 0.95
ENTROPY_COEF = 0.05

BF = jnp.bfloat16
F32 = jnp.float32
ROWS = 256
WIN = 128
OUTS = 544
NEG = -1e30
MESH = pl.DeviceIdType.MESH


def dot_nn(left, right):
    return jnp.dot(left, right, preferred_element_type=F32)


def dot_tn(left, right):
    return lax.dot_general(left, right, (((0,), (0,)), ((), ())), preferred_element_type=F32)


def dot_nt(left, right):
    return lax.dot_general(left, right, (((1,), (1,)), ((), ())), preferred_element_type=F32)


def iota(shape, dim):
    return lax.broadcasted_iota(jnp.int32, shape, dim)


def rms_apply(x, gain):
    inv = lax.rsqrt(jnp.mean(x * x, axis=-1, keepdims=True) + EPS_NORM)
    return (x * inv * gain).astype(BF)


def rms_pull(grad, x, gain):
    inv = lax.rsqrt(jnp.mean(x * x, axis=-1, keepdims=True) + EPS_NORM)
    unit = x * inv
    weighted = grad * gain
    grad_x = inv * (weighted - unit * jnp.mean(weighted * unit, axis=-1, keepdims=True))
    rows, dims = x.shape
    return grad_x, jnp.sum((grad * unit).reshape(rows // 8, 8, dims), axis=0)


def step_kernel(
    layers,
    seq_size,
    codes_ref,
    actions_ref,
    next_ref,
    lengths_ref,
    rewards_ref,
    continues_ref,
    values_ref,
    freq_ref,
    table_ref,
    attn_in_ref,
    attn_out_ref,
    ffn_in_ref,
    ffn_out_ref,
    gains_ref,
    readout_ref,
    grads_ref,
    scal_ref,
    wq,
    wo,
    wu,
    wd,
    rt,
    tb,
    xs,
    hs,
    qs,
    kvs,
    probs,
    acts,
    gds,
    mixes,
    bias,
    tokf,
    toki,
    gouts,
    gx,
    gl,
    dmix,
    dqkv,
    dkv,
    dgain,
    lossacc,
    lam,
    ang,
    bsend,
    brecv,
    send_sem,
    recv_sem,
    load_sem,
):
    batch, span = codes_ref.shape
    dims = gains_ref.shape[1]
    ff = ffn_in_ref.shape[2]
    tiles = span // SEG
    total = batch * span
    chunks = total // ROWS
    per_seq = span // ROWS
    vocab_all = table_ref.shape[0]
    outs_all = readout_ref.shape[1]
    head_dim = dims // HEADS
    scale = head_dim ** (-0.5)
    exp_scale = scale * math.log2(math.e)
    groups = HEADS // 2
    base = lax.axis_index("seq") * span
    me = lax.axis_index("seq")
    right = lax.rem(me + 1, seq_size)
    left = lax.rem(me + seq_size - 1, seq_size)

    barrier = pltpu.get_barrier_semaphore()
    for neighbour in (left, right):
        pl.semaphore_signal(barrier, inc=1, device_id={"seq": neighbour}, device_id_type=MESH)
    pl.semaphore_wait(barrier, 2)

    blocks = []
    for layer in range(layers):
        for j in range(3):
            blocks.append((attn_in_ref, wq, layer, slice(0, 256), slice(j * 256, j * 256 + 256)))
        blocks.append((attn_out_ref, wo, layer, slice(0, 256), slice(0, 256)))
        for j in range(ff // 256):
            blocks.append((ffn_in_ref, wu, layer, slice(0, 256), slice(j * 256, j * 256 + 256)))
        for j in range(ff // 256):
            blocks.append((ffn_out_ref, wd, layer, slice(j * 256, j * 256 + 256), slice(0, 256)))

    def block_copy(k):
        source, _, layer, rows, cols = blocks[k]
        at = 256 * (k % chunks)
        return pltpu.make_async_copy(
            source.at[layer, rows, cols], xs.at[1 + k // chunks, at : at + 256, :], load_sem.at[k]
        )

    for k in range(len(blocks)):
        block_copy(k).start()
    tb[...] = jnp.zeros_like(tb)
    tb[0:vocab_all, :] = table_ref[...].astype(BF)
    for part in range(VOCAB // 256):
        rt[part * 256 : part * 256 + 256, :] = readout_ref[:, part * 256 : part * 256 + 256].T.astype(BF)
    rest = outs_all - VOCAB
    tail = jnp.concatenate(
        [readout_ref[:, VOCAB:outs_all], jnp.zeros((dims, 128 - rest), F32)], axis=1
    ).T
    rt[VOCAB:OUTS, :] = tail[0 : OUTS - VOCAB].astype(BF)

    ends = []
    for b in range(batch):
        run = jnp.int32(0)
        row = []
        for e in range(lengths_ref.shape[1]):
            run = run + lengths_ref[b, e]
            row.append(run)
        ends.append(row)
    episodes = len(ends[0])

    lane = iota((8, span), 1)
    lam[...] = jnp.zeros_like(lam)
    lam[0, 0:batch, :] = rewards_ref[...]
    lam[1, 0:batch, :] = continues_ref[...]
    lam[2, 0:batch, :] = values_ref[...]
    last = lax.rem(lane, SEG) == SEG - 1
    decay = GAMMA * lam[1]
    value_next = pltpu.roll(lam[2], span - 1, 1)
    add = jnp.where(last, lam[2], lam[0] + decay * ((1.0 - LAMBDA_RET) * value_next))
    mul = jnp.where(last, 0.0, decay * LAMBDA_RET)
    step = 1
    while step < SEG:
        add = add + mul * pltpu.roll(add, span - step, 1)
        mul = mul * pltpu.roll(mul, span - step, 1)
        step *= 2
    lam[3] = add
    valid_rows = []
    for b in range(batch):
        after = iota((1, span), 1) + (base + 1)
        final = after == ends[b][0]
        for e in range(1, episodes):
            final = final | (after == ends[b][e])
        valid_rows.append(jnp.where(final, 0.0, 1.0))
    for c in range(chunks):
        b = c // per_seq
        lanes = slice((c % per_seq) * ROWS, (c % per_seq) * ROWS + ROWS)
        for row in range(4):
            tokf[c, row : row + 1, :] = lam[row, b : b + 1, lanes]
        tokf[c, 4:5, :] = valid_rows[b][:, lanes]
        toki[c, 0:1, :] = codes_ref[b : b + 1, lanes]
        toki[c, 1:2, :] = actions_ref[b : b + 1, lanes]
        toki[c, 2:3, :] = next_ref[b : b + 1, lanes]

    half = dims // 2
    freq = freq_ref[...]
    in_angle = iota((SEG, half), 0).astype(F32) * freq
    in_sin, in_cos = jnp.sin(in_angle), jnp.cos(in_angle)
    tile_angle = (iota((tiles, half), 0) * SEG + base).astype(F32) * freq
    all_sin, all_cos = jnp.sin(tile_angle), jnp.cos(tile_angle)
    for tile in range(tiles):
        ang[tile, 0:1, :] = all_sin[tile : tile + 1, :]
        ang[tile, 1:2, :] = all_cos[tile : tile + 1, :]
    end_row = iota((batch * episodes, half), 0)
    end_all = jnp.zeros((batch * episodes, half), jnp.int32)
    for b in range(batch):
        for e in range(episodes):
            end_all = jnp.where(end_row == b * episodes + e, ends[b][e], end_all)
    end_angle = end_all.astype(F32) * freq
    end_sin, end_cos = jnp.sin(end_angle), jnp.cos(end_angle)

    def marks(tile, carry):
        tile_sin = ang[tile, 0:1, :]
        tile_cos = ang[tile, 1:2, :]
        here_sin = in_sin * tile_cos + in_cos * tile_sin
        here_cos = in_cos * tile_cos - in_sin * tile_sin
        place = iota((SEG, half), 0) + (base + tile * SEG)
        key_place = iota((SEG, WIN), 1) + (base + tile * SEG - SEG)
        for b in range(batch):
            start = jnp.zeros((SEG, half), jnp.int32)
            start_sin = jnp.zeros((SEG, half), F32)
            start_cos = jnp.ones((SEG, half), F32)
            for e in range(episodes):
                passed = place >= ends[b][e]
                row = b * episodes + e
                start = jnp.where(passed, ends[b][e], start)
                start_sin = jnp.where(passed, end_sin[row : row + 1, :], start_sin)
                start_cos = jnp.where(passed, end_cos[row : row + 1, :], start_cos)
            rows = pl.ds(pl.multiple_of(b * span + tile * SEG, SEG), SEG)
            xs[0, rows, 0:half] = here_sin * start_cos - here_cos * start_sin
            xs[0, rows, half:dims] = here_cos * start_cos + here_sin * start_sin
            seen = (key_place <= place) & (key_place >= start)
            bias[rows, :] = jnp.where(seen, 0.0, NEG)
        return carry

    lax.fori_loop(0, tiles, marks, 0)

    for layer in range(layers):
        for b in range(batch):
            kvs[layer, b, SEG + span :, :] = jnp.zeros((kvs.shape[2] - SEG - span, 2 * dims), BF)

    def chunk_rows(c):
        return pl.ds(pl.multiple_of(c * ROWS, ROWS), ROWS)

    def kv_rows(c):
        return pl.ds(pl.multiple_of(lax.rem(c, per_seq) * ROWS + SEG, 16), ROWS)

    for k, (_, dest, layer, rows, cols) in enumerate(blocks):
        block_copy(k).wait()
        at = 256 * (k % chunks)
        dest[layer, rows, cols] = xs[1 + k // chunks, at : at + 256, :].astype(BF)

    def onehot(c):
        code = toki[c, 0:1, :]
        act = toki[c, 1:2, :] + VOCAB
        ids = iota((OUTS, ROWS), 0)
        return jnp.where((ids == code) | (ids == act), 1.0, 0.0).astype(BF)

    def embed(c, carry):
        rows = chunk_rows(c)
        xs[0, rows, :] += dot_tn(onehot(c), tb[...])
        return carry

    lax.fori_loop(0, chunks, embed, 0)

    lane_head = iota((1, dims), 1) // head_dim
    group_mask = [jnp.where(lane_head // 2 == g, 1.0, 0.0).astype(BF) for g in range(groups)]
    even_mask = jnp.where(lax.rem(lane_head, 2) == 0, 1.0, 0.0).astype(BF)
    odd_mask = jnp.where(lax.rem(lane_head, 2) == 1, 1.0, 0.0).astype(BF)
    even_f = lax.rem(lane_head, 2) == 0

    def spread(rows):
        return jnp.concatenate([rows * group_mask[g] for g in range(groups)], axis=0)

    def both(keys):
        return jnp.concatenate([keys * even_mask, keys * odd_mask], axis=0)

    def gather_heads(wide):
        out = wide[0:SEG]
        for g in range(1, groups):
            out = jnp.where(lane_head // 2 == g, wide[g * SEG : g * SEG + SEG], out)
        return out

    def forward_copy(layer):
        return pltpu.make_async_remote_copy(
            src_ref=kvs.at[layer, :, pl.ds(span, SEG), :],
            dst_ref=kvs.at[layer, :, pl.ds(0, SEG), :],
            send_sem=send_sem.at[layer],
            recv_sem=recv_sem.at[layer],
            device_id={"seq": right},
            device_id_type=MESH,
        )

    def backward_copy(layer):
        return pltpu.make_async_remote_copy(
            src_ref=bsend.at[layer],
            dst_ref=brecv.at[layer],
            send_sem=send_sem.at[layers + layer],
            recv_sem=recv_sem.at[layers + layer],
            device_id={"seq": left},
            device_id_type=MESH,
        )

    def project(layer):
        def body(c, carry):
            rows = chunk_rows(c)
            h = rms_apply(xs[2 * layer, rows, :], gains_ref[2 * layer : 2 * layer + 1, :])
            hs[2 * layer, rows, :] = h
            qkv = dot_nn(h, wq[layer]).astype(BF)
            qs[layer, rows, :] = qkv[:, 0:dims]
            kvs[layer, c // per_seq, kv_rows(c), :] = qkv[:, dims:]
            return carry

        lax.fori_loop(0, chunks, body, 0)

    def attend(layer):
        def one(b, tile):
            rows = pl.ds(pl.multiple_of(b * span + tile * SEG, SEG), SEG)
            window = pl.ds(pl.multiple_of(tile * SEG, SEG), WIN)
            keys = kvs[layer, b, window, 0:dims]
            values = kvs[layer, b, window, dims:]
            mask = bias[rows, :]
            mask = jnp.concatenate([mask] * groups, axis=0)
            scores = dot_nt(spread(qs[layer, rows, :]), both(keys))
            sides = []
            for side in range(2):
                s = scores[:, side * WIN : side * WIN + WIN] + mask
                top = jnp.max(s, axis=-1, keepdims=True)
                e = jnp.exp2((s - top) * exp_scale)
                sides.append((e / jnp.sum(e, axis=-1, keepdims=True)).astype(BF))
            p = jnp.concatenate(sides, axis=1)
            probs[layer, b * tiles + tile] = p
            wide = dot_nn(p, both(values))
            mixes[layer, rows, :] = gather_heads(wide).astype(BF)

        def body(i, carry):
            tile = tiles - 1 - i
            for b in range(batch):
                one(b, tile)
            return carry

        copy = forward_copy(layer)
        copy.start()
        lax.fori_loop(0, tiles - 1, body, 0)
        copy.wait()
        lax.fori_loop(tiles - 1, tiles, body, 0)

    def feed(layer):
        def body(c, carry):
            rows = chunk_rows(c)
            x = xs[2 * layer, rows, :] + dot_nn(mixes[layer, rows, :], wo[layer])
            xs[2 * layer + 1, rows, :] = x
            h = rms_apply(x, gains_ref[2 * layer + 1 : 2 * layer + 2, :])
            hs[2 * layer + 1, rows, :] = h
            for j in range(ff // 256):
                cols = slice(j * 256, j * 256 + 256)
                up = dot_nn(h, wu[layer, :, cols])
                square = up * up
                c0 = math.sqrt(2.0 / math.pi)
                t = jnp.tanh(c0 * up * (1.0 + 0.044715 * square))
                half_t = 0.5 * (1.0 + t)
                acts[layer, rows, cols] = (up * half_t).astype(BF)
                slope = half_t + (0.5 * c0) * up * (1.0 - t * t) * (1.0 + (3.0 * 0.044715) * square)
                gds[layer, rows, cols] = slope.astype(BF)
            xs[2 * layer + 2, rows, :] = x + dot_nn(acts[layer, rows, :], wd[layer])
            return carry

        lax.fori_loop(0, chunks, body, 0)

    for layer in range(layers):
        project(layer)
        attend(layer)
        feed(layer)

    lossacc[...] = jnp.zeros_like(lossacc)
    dgain[...] = jnp.zeros_like(dgain)
    top_gain = gains_ref[2 * layers : 2 * layers + 1, :]

    def losses(c, carry):
        rows = chunk_rows(c)
        x = xs[2 * layers, rows, :]
        h = rms_apply(x, top_gain)
        hs[2 * layers, rows, :] = h
        outs = dot_nt(rt[...], h)
        reward, cont = tokf[c, 0:1, :], tokf[c, 1:2, :]
        target, ret, valid = tokf[c, 2:3, :], tokf[c, 3:4, :], tokf[c, 4:5, :]
        action, code = toki[c, 1:2, :], toki[c, 2:3, :]
        logits = outs[0:VOCAB]
        top = jnp.max(logits, axis=0, keepdims=True)
        e = jnp.exp(logits - top)
        esum = jnp.sum(e, axis=0, keepdims=True)
        chosen = iota((VOCAB, ROWS), 0) == code
        picked = jnp.sum(jnp.where(chosen, logits, 0.0), axis=0, keepdims=True)
        loss = jnp.log(esum) + top - picked
        gouts[0:VOCAB, rows] = (e * (valid / esum) - jnp.where(chosen, valid, 0.0)).astype(BF)
        small = outs[VOCAB:OUTS]
        place = iota((OUTS - VOCAB, ROWS), 0)
        reward_err = small[0:1] - reward
        end_logit = small[1:2]
        value_err = small[2:3] - ret
        minus = jnp.exp(-jnp.abs(end_logit))
        soft = jnp.maximum(end_logit, 0.0) + jnp.log(1.0 + minus)
        sigmoid = jnp.where(end_logit >= 0.0, 1.0, minus) / (1.0 + minus)
        loss = loss + 0.5 * reward_err * reward_err + soft - cont * end_logit
        loss = loss + 0.5 * value_err * value_err
        actor = (place >= 3) & (place < outs_all - VOCAB)
        act_top = jnp.max(jnp.where(actor, small, NEG), axis=0, keepdims=True)
        act_e = jnp.where(actor, jnp.exp(jnp.where(actor, small - act_top, 0.0)), 0.0)
        act_sum = jnp.sum(act_e, axis=0, keepdims=True)
        log_pi = jnp.where(actor, small - act_top - jnp.log(act_sum), 0.0)
        pi = act_e / act_sum
        neg_entropy = jnp.sum(pi * log_pi, axis=0, keepdims=True)
        taken = place == action + 3
        picked_pi = jnp.sum(jnp.where(taken, log_pi, 0.0), axis=0, keepdims=True)
        gap = ret - target
        loss = loss - gap * picked_pi + ENTROPY_COEF * neg_entropy
        grad = gap * (pi - jnp.where(taken, 1.0, 0.0))
        grad = grad + ENTROPY_COEF * pi * (log_pi - neg_entropy)
        grad = jnp.where(actor, grad, 0.0)
        grad = jnp.where(place == 0, reward_err, grad)
        grad = jnp.where(place == 1, sigmoid - cont, grad)
        grad = jnp.where(place == 2, value_err, grad)
        gouts[VOCAB:OUTS, rows] = (grad * valid).astype(BF)
        lossacc[0:1, :] += loss * valid
        lossacc[1:2, :] += valid
        dh = dot_tn(gouts[:, rows], rt[...])
        grad_x, part = rms_pull(dh, x, top_gain)
        gx[rows, :] = grad_x
        dgain[2 * layers] += part
        return carry

    lax.fori_loop(0, chunks, losses, 0)
    grads_ref[0:OUTS, :] = dot_nn(gouts[...], hs[2 * layers]).astype(BF)
    loss_total = jnp.sum(lossacc[0:1, :])
    count_total = jnp.sum(lossacc[1:2, :])
    place = iota(scal_ref.shape, 0)
    scal_ref[...] = jnp.where(place == 0, loss_total, jnp.where(place == 1, count_total, 0.0))

    def feed_back(layer):
        def body(c, carry):
            rows = chunk_rows(c)
            grad = gx[rows, :]
            low = grad.astype(BF)
            gl[rows, :] = low
            for j in range(ff // 256):
                cols = slice(j * 256, j * 256 + 256)
                da = dot_nt(low, wd[layer, cols, :])
                gds[layer, rows, cols] = (da * gds[layer, rows, cols].astype(F32)).astype(BF)
            dh = dot_nt(gds[layer, rows, :], wu[layer])
            gain = gains_ref[2 * layer + 1 : 2 * layer + 2, :]
            grad_x, part = rms_pull(dh, xs[2 * layer + 1, rows, :], gain)
            dgain[2 * layer + 1] += part
            grad = grad + grad_x
            gx[rows, :] = grad
            dmix[rows, :] = dot_nt(grad.astype(BF), wo[layer]).astype(BF)
            return carry

        lax.fori_loop(0, chunks, body, 0)

    def attend_back(layer):
        def one(b, tile):
            rows = pl.ds(pl.multiple_of(b * span + tile * SEG, SEG), SEG)
            window = pl.ds(pl.multiple_of(tile * SEG, SEG), WIN)
            keys = both(kvs[layer, b, window, 0:dims])
            values = both(kvs[layer, b, window, dims:])
            queries = spread(qs[layer, rows, :])
            dout = spread(dmix[rows, :])
            p = probs[layer, b * tiles + tile]
            dp = dot_nt(dout, values)
            sides = []
            for side in range(2):
                cols = slice(side * WIN, side * WIN + WIN)
                pf = p[:, cols].astype(F32)
                d = dp[:, cols]
                sides.append((pf * (d - jnp.sum(d * pf, axis=-1, keepdims=True))).astype(BF))
            ds = jnp.concatenate(sides, axis=1)
            dq = gather_heads(dot_nn(ds, keys)) * scale
            dqkv[rows, 0:dims] = dq.astype(BF)
            dk = dot_tn(ds, queries) * scale
            dk = jnp.where(even_f, dk[0 : 2 * SEG], dk[WIN : WIN + 2 * SEG])
            dv = dot_tn(p, dout)
            dv = jnp.where(even_f, dv[0 : 2 * SEG], dv[WIN : WIN + 2 * SEG])
            old = pl.ds(pl.multiple_of(tile * SEG, SEG), SEG)
            new = pl.ds(pl.multiple_of(tile * SEG + SEG, SEG), SEG)
            dkv[b, old, 0:dims] += dk[0:SEG]
            dkv[b, old, dims:] += dv[0:SEG]
            dkv[b, new, 0:dims] = dk[SEG:]
            dkv[b, new, dims:] = dv[SEG:]

        def body(tile, carry):
            for b in range(batch):
                one(b, tile)
            return carry

        for b in range(batch):
            dkv[b, 0:SEG, :] = jnp.zeros((SEG, 2 * dims), F32)
        lax.fori_loop(0, 1, body, 0)
        for b in range(batch):
            bsend[layer, b] = dkv[b, 0:SEG, :].astype(BF)
        copy = backward_copy(layer)
        copy.start()
        lax.fori_loop(1, tiles, body, 0)
        copy.wait()
        for b in range(batch):
            dkv[b, span : span + SEG, :] += brecv[layer, b].astype(F32)

    def project_back(layer):
        def body(c, carry):
            rows = chunk_rows(c)
            dqkv[rows, dims:] = dkv[c // per_seq, kv_rows(c), :].astype(BF)
            dh = dot_nt(dqkv[rows, :], wq[layer])
            gain = gains_ref[2 * layer : 2 * layer + 1, :]
            grad_x, part = rms_pull(dh, xs[2 * layer, rows, :], gain)
            dgain[2 * layer] += part
            gx[rows, :] += grad_x
            return carry

        lax.fori_loop(0, chunks, body, 0)

    at = OUTS
    for layer in reversed(range(layers)):
        feed_back(layer)
        for j in range(ff // 256):
            cols = slice(j * 256, j * 256 + 256)
            grads_ref[at : at + 256, :] = dot_tn(acts[layer, :, cols], gl[...]).astype(BF)
            at += 256
        for j in range(ff // 256):
            cols = slice(j * 256, j * 256 + 256)
            grads_ref[at : at + 256, :] = dot_tn(hs[2 * layer + 1], gds[layer, :, cols]).astype(BF)
            at += 256
        gl[...] = gx[...].astype(BF)
        grads_ref[at : at + 256, :] = dot_tn(mixes[layer], gl[...]).astype(BF)
        at += 256
        attend_back(layer)
        project_back(layer)
        for j in range(3):
            cols = slice(j * 256, j * 256 + 256)
            grads_ref[at : at + 256, :] = dot_tn(hs[2 * layer], dqkv[:, cols]).astype(BF)
            at += 256
    gl[...] = gx[...].astype(BF)

    def mark(c, carry):
        gouts[:, chunk_rows(c)] = onehot(c)
        return carry

    lax.fori_loop(0, chunks, mark, 0)
    grads_ref[at : at + OUTS, :] = dot_nn(gouts[...], gl[...]).astype(BF)
    at += OUTS
    place = iota((16, dims), 0)
    gain_rows = jnp.zeros((16, dims), F32)
    for index in range(2 * layers + 1):
        gain_rows = jnp.where(place == index, jnp.sum(dgain[index], axis=0, keepdims=True), gain_rows)
    grads_ref[at : at + 16, :] = gain_rows.astype(BF)


def gradients(codes, actions, next_codes, lengths, rewards, continues, values, weights, seq_size):
    table, attn_in, attn_out, ffn_in, ffn_out, gains, readout = weights
    batch, span = codes.shape
    layers, dims, ff = ffn_in.shape
    total = batch * span
    tiles = span // SEG
    chunks = total // ROWS
    grad_rows = 2 * OUTS + layers * 12 * 256 + 16
    freq = jnp.exp(
        jnp.arange(dims // 2).astype(F32) * (-2.0 * math.log(10000.0) / dims)
    )[None, :]
    vmem = pl.BlockSpec(memory_space=pltpu.VMEM)
    smem = pl.BlockSpec(memory_space=pltpu.SMEM)
    kv_span = -(-(span - SEG + WIN) // 16) * 16
    return pl.pallas_call(
        functools.partial(step_kernel, layers, seq_size),
        out_shape=(
            jax.ShapeDtypeStruct((grad_rows, dims), BF),
            jax.ShapeDtypeStruct((8, 128), F32),
        ),
        in_specs=[vmem] * 3 + [smem] + [vmem] * 5 + [pl.BlockSpec(memory_space=pl.ANY)] * 4 + [vmem] * 2,
        out_specs=(vmem, vmem),
        scratch_shapes=[
            pltpu.VMEM((layers, dims, 3 * dims), BF),
            pltpu.VMEM((layers, dims, dims), BF),
            pltpu.VMEM((layers, dims, ff), BF),
            pltpu.VMEM((layers, ff, dims), BF),
            pltpu.VMEM((OUTS, dims), BF),
            pltpu.VMEM((OUTS, dims), BF),
            pltpu.VMEM((2 * layers + 1, total, dims), F32),
            pltpu.VMEM((2 * layers + 1, total, dims), BF),
            pltpu.VMEM((layers, total, dims), BF),
            pltpu.VMEM((layers, batch, kv_span, 2 * dims), BF),
            pltpu.VMEM((layers, batch * tiles, HEADS // 2 * SEG, 2 * WIN), BF),
            pltpu.VMEM((layers, total, ff), BF),
            pltpu.VMEM((layers, total, ff), BF),
            pltpu.VMEM((layers, total, dims), BF),
            pltpu.VMEM((total, WIN), F32),
            pltpu.VMEM((chunks, 8, ROWS), F32),
            pltpu.VMEM((chunks, 8, ROWS), jnp.int32),
            pltpu.VMEM((OUTS, total), BF),
            pltpu.VMEM((total, dims), F32),
            pltpu.VMEM((total, dims), BF),
            pltpu.VMEM((total, dims), BF),
            pltpu.VMEM((total, 3 * dims), BF),
            pltpu.VMEM((batch, SEG + span, 2 * dims), F32),
            pltpu.VMEM((2 * layers + 1, 8, dims), F32),
            pltpu.VMEM((8, ROWS), F32),
            pltpu.VMEM((4, 8, span), F32),
            pltpu.VMEM((tiles, 8, dims // 2), F32),
            pltpu.VMEM((layers, batch, SEG, 2 * dims), BF),
            pltpu.VMEM((layers, batch, SEG, 2 * dims), BF),
            pltpu.SemaphoreType.DMA((2 * layers,)),
            pltpu.SemaphoreType.DMA((2 * layers,)),
            pltpu.SemaphoreType.DMA((12 * layers,)),
        ],
        compiler_params=pltpu.CompilerParams(
            collective_id=0, has_side_effects=True, vmem_limit_bytes=63 * 1024 * 1024
        ),
        name="train_step",
    )(
        codes,
        actions,
        next_codes,
        lengths,
        rewards,
        continues,
        values,
        freq,
        table,
        attn_in,
        attn_out,
        ffn_in,
        ffn_out,
        gains,
        readout,
    )


def adam_update(weight, first_mom, second_mom, clipped, rate):
    new_first = BETA_ONE * first_mom + (1.0 - BETA_ONE) * clipped
    new_second = BETA_TWO * second_mom + (1.0 - BETA_TWO) * clipped * clipped
    ratio = (
        new_first
        / (1.0 - BETA_ONE**STEP)
        / (jnp.sqrt(new_second / (1.0 - BETA_TWO**STEP)) + ADAM_EPS)
    )
    return (weight - rate * (ratio + DECAY * weight), new_first, new_second)


def unpack(grads, weights):
    table, attn_in, attn_out, ffn_in, ffn_out, gains, readout = weights
    layers, dims, ff = ffn_in.shape
    read = grads[0:OUTS].T[:, : readout.shape[1]]
    at = OUTS
    per_layer = [None] * layers
    for layer in reversed(range(layers)):
        down = grads[at : at + ff]
        at += ff
        up = grads[at : at + ff].reshape(ff // 256, dims, 256).transpose(1, 0, 2).reshape(dims, ff)
        at += ff
        out = grads[at : at + dims]
        at += dims
        qkv = grads[at : at + 3 * dims].reshape(3, dims, 256).transpose(1, 0, 2).reshape(dims, 3 * dims)
        at += 3 * dims
        per_layer[layer] = (qkv, out, up, down)
    tab = grads[at : at + table.shape[0]]
    at += OUTS
    gain = grads[at : at + gains.shape[0]]
    stacked = [jnp.stack([entry[k] for entry in per_layer]) for k in range(4)]
    return (tab, *stacked, gain, read)


def local(codes, actions, next_codes, lengths, rewards, continues, target_values, *state):
    params, firsts, seconds = state[0::3], state[1::3], state[2::3]
    grads, scal = gradients(
        codes,
        actions,
        next_codes,
        lengths,
        rewards,
        continues,
        target_values,
        params,
        lax.axis_size("seq"),
    )
    grads = lax.psum(grads, ("seq", "dp")).astype(F32)
    scal = lax.psum(scal, ("seq", "dp"))
    loss_sum, step_count = scal[0, 0], scal[1, 0]
    averaged = [grad / step_count for grad in unpack(grads, params)]
    grad_norm = jnp.sqrt(sum((jnp.sum(grad * grad) for grad in averaged)))
    factor = jnp.minimum(1.0, CLIP_NORM / grad_norm)
    results = []
    for slot in range(7):
        results.extend(
            adam_update(
                params[slot], firsts[slot], seconds[slot], averaged[slot] * factor, RATES[slot]
            )
        )
    return tuple(results) + (loss_sum, step_count, grad_norm)


def solution(mesh):
    rows, whole = P("dp", "seq"), P()
    return jax.shard_map(
        local,
        mesh=mesh,
        in_specs=(rows, rows, rows, P("dp", None), rows, rows, rows) + (whole,) * 21,
        out_specs=(whole,) * 24,
        check_vma=False,
    )
```

time: 688 us -> 351 us (0.51)
  local copies, waits for them, and re-layouts: 207 us -> 32.5 us
  blocking collectives: 161 us -> 39.6 us
  Pallas kernels: 0 us -> 120 us
  matrix products: 115 us -> 0 us
  other arithmetic: 99.3 us -> 45 us
  waiting for transfers between devices: 62.9 us -> 93.2 us
  starting transfers between devices: 12.1 us -> 0.04 us
    psum x2 -> x1, blocking collectives: 161 us -> 39.6 us  [local(): scal = lax.psum(scal, ('seq', 'dp'))]
    pallas_call x0 -> x1, Pallas kernels: none -> 120 us  [gradients(): pl.pallas_call(functools.partial(step_kernel, layers, seq_size), out_shap...]
    dot_general x39 -> x0, matrix products: 96.3 us -> none  [the longest x9 23 us: matmul_right(): lax.dot_general(left, right, (((1,), (1,)), ((), ())), preferred_element_...]
    reshape x23 -> x2, local copies, waits for them, and re-layouts: 58.3 us -> 2.3 us  [unpack(): grads[at:at + 3 * dims].reshape(3, dims, 256).transpose(1, 0, 2)]
    psum x1, waiting for transfers between devices: 60.7 us -> 93.2 us  [local(): grads = lax.psum(grads, ('seq', 'dp')).astype(F32)]
    concatenate x10 -> x0, local copies, waits for them, and re-layouts: 32.5 us -> none  [the longest x4 15.2 us: layer_forward(): jnp.concatenate([prev_values, own_values], axis=2)]
    slice x23 -> x3, local copies, waits for them, and re-layouts: 33.3 us -> 4.08 us  [the longest x1 2.33 us: unpack(): grads[at:at + ff].reshape(ff // 256, dims, 256).transpose(1, 0, 2)]
    another operation x16 -> x0, other arithmetic: 26.5 us -> none
  transfers between devices with their start and end apart: 5 -> 1, of which waited for: 2 -> 1; matrix products, arithmetic and copies ran while one was open for 17% -> 2% of each run, Pallas kernels for 0% -> 0%
where the time goes in v1:
time: 351 us; the launch traced here: 350 us
  Pallas kernels  120 us (34%)
  waiting for transfers between devices  93.2 us (27%)
  other arithmetic  45 us (13%)
  blocking collectives  39.6 us (11%)
  local copies, waits for them, and re-layouts  32.5 us (9%)
  between operations  20 us (6%)
    pallas_call x1, Pallas kernels, gradients(): pl.pallas_call(functools.partial(step_kernel, layers, seq_size), out_shap...  120 us
    psum x1, waiting for transfers between devices, local(): grads = lax.psum(grads, ('seq', 'dp')).astype(F32)  93.2 us
    psum x1, blocking collectives, local(): scal = lax.psum(scal, ('seq', 'dp'))  39.6 us
    sub x7, other arithmetic, adam_update(): return (weight - rate * (ratio + DECAY * weight), new_first, new_second)  26 us
    unnamed x53, local copies, waits for them, and re-layouts  17.6 us
    reduce_sum x7, other arithmetic, local(): grad_norm = jnp.sqrt(sum((jnp.sum(grad * grad) for grad in averaged)))  15.8 us
  transfers between devices with their start and end apart: 1, of which 1 were waited for; matrix products, arithmetic and copies ran while one was open for 2% of the time, Pallas kernels for 0%

profile of v1, /device:TPU:0, one launch (start us, length us, event | category | flops | bytes accessed | tf_op | source)
XLA Modules:
  0.0 350.0 jit_solution(14054653902201360786)
XLA Ops:
  7.8 2.1 copy.57.readout_ref
  9.9 119.8 %train_step.1 = (bf16[7248,256]{1,0:T(8,128)(2,1)}, f32[8,128]{1,0:T(8,128)}) custom-call(s32[2,768]{1,0:T(2,128)} %codes_ref.1, s32[2,768]{1,0:T(2,128)} %actions_ref.1, s32[2,768]{1,0:T(2,128)} %next_ref.1, s32[2,8]{1,0:T(2,128)} %lengths_ref.1, f32[2,768]{1,0:T(2,128)} %rewards_ref.1, f32[2,768]{1,0:T(2,128)} %continues_ref.1, f32[2,768]{1,0:T(2,128)} %values_ref.1, ...), custom_call_target="tpu_custom_call" | custom-call | tf_op jit(solution)/shard_map/train_step/pallas_call | solution.py:589
  129.7 1.4 copy-done.4
  131.1 1.6 copy.65
  132.7 1.6 copy.62
  134.3 1.6 copy.63
  135.9 39.6 %psum.15 = f32[8,128]{1,0:T(8,128)S(1)} all-reduce(f32[8,128]{1,0:T(8,128)S(1)} %copy-done.22), channel_id=1, replica_groups=mesh['seq'=4,'dp'=8] {'seq','dp'}, use_global_device_ids=true, to_apply=%region_1.0 | all-reduce | flops 1024 | bytes 8192 | tf_op jit(solution)/shard_map/psum | solution.py:702
  176.0 93.2 %all-reduce.2.cloned.1.call-done = bf16[7248,256]{1,0:T(8,128)(2,1)} async-done(((bf16[7248,256]{1,0:T(8,128)(2,1)}), bf16[7248,256]{1,0:T(8,128)(2,1)}) %all-reduce.2.cloned.1.call-update) | async-done | bytes 3710992 | tf_op jit(solution)/shard_map/psum | solution.py:701
  269.2 2.6 convert_element_type.14
  271.9 1.7 multiply_reduce_fusion.6
  273.6 1.4 multiply_reduce_fusion.4
  277.7 1.2 fusion.15
  278.9 1.1 copy.58
  280.1 1.1 copy.59
  281.2 2.3 fusion.14
  284.8 2.9 copy.61
  287.7 1.8 stack_reshape.15
  289.4 2.4 multiply_reduce_fusion.3
  291.9 3.0 multiply_reduce_fusion.2
  294.9 1.8 multiply_reduce_fusion.1
  298.0 2.3 multiply_reduce_fusion.5
  301.6 3.0 multiply_reduce_fusion
  306.7 6.4 %multiply_subtract_fusion.2 = (f32[2,256,768]{1,2,0:T(8,128)}, f32[2,256,768]{1,2,0:T(8,128)}, f32[2,256,768]{1,2,0:T(8,128)}) fusion(f32[2,256,768]{1,2,0:T(8,128)} %copy.65, f32[]{:T(128)S(6)} %min_shard_map.3, f32[]{:T(128)} %bitcast, f32[1,256,768]{1,2,0:T(8,128)} %bitcast.29, f32[1,256,768]{1,2,0:T(8,128)} %bitcast.27, f32[2,256,768]{1,2,0:T(8,128)} %copy.62, ...), kind=kLoop, calls=%fused_computation.15 | loop fusion | flops 7077888 | bytes 11010056 | tf_op jit(solution)/shard_map/sub | solution.py:662
  313.1 3.0 copy.66
  316.1 3.0 copy.67
  319.2 3.1 copy.68
  322.3 2.1 multiply_subtract_fusion.6
  324.4 3.9 %multiply_subtract_fusion.4 = (f32[530,256]{1,0:T(8,128)}, f32[530,256]{1,0:T(8,128)}, f32[530,256]{1,0:T(8,128)}) fusion(f32[530,256]{1,0:T(8,128)} %table_ref.1, f32[]{:T(128)S(6)} %min_shard_map.3, f32[]{:T(128)} %bitcast, f32[7248,256]{1,0:T(8,128)} %copy-done, f32[530,256]{1,0:T(8,128)} %param.36, f32[530,256]{1,0:T(8,128)} %param.37), kind=kLoop, calls=%fused_computation.30 | loop fusion | flops 2306560 | bytes 3799048 | tf_op jit(solution)/shard_map/sub | solution.py:662
  328.4 2.2 multiply_subtract_fusion.5
  330.7 2.3 multiply_subtract_fusion.3
  333.0 4.5 %multiply_subtract_fusion = (f32[2,1024,256]{2,1,0:T(8,128)}, f32[2,1024,256]{2,1,0:T(8,128)}, f32[2,1024,256]{2,1,0:T(8,128)}) fusion(f32[2,1024,256]{2,1,0:T(8,128)S(1)} %copy-done.2, f32[]{:T(128)S(6)} %min_shard_map.3, f32[]{:T(128)} %bitcast, f32[1,1024,256]{2,1,0:T(8,128)S(1)} %copy-done.1, f32[1,1024,256]{2,1,0:T(8,128)S(1)} %get-tuple-element.73, ...), kind=kLoop, calls=%fused_computation.7 | loop fusion | flops 9437184 | bytes 14680072 | tf_op jit(solution)/shard_map/sub | solution.py:662
  337.5 4.5 %multiply_subtract_fusion.1 = (f32[2,256,1024]{2,1,0:T(8,128)}, f32[2,256,1024]{2,1,0:T(8,128)}, f32[2,256,1024]{2,1,0:T(8,128)}) fusion(f32[2,256,1024]{2,1,0:T(8,128)S(1)} %copy-done.3, f32[]{:T(128)S(6)} %min_shard_map.3, f32[]{:T(128)} %bitcast, f32[1,256,1024]{2,1,0:T(8,128)S(1)} %stack_reshape.15, f32[1,256,1024]{2,1,0:T(8,128)S(1)} %stack_reshape.14, ...), kind=kLoop, calls=%fused_computation.9 | loop fusion | flops 9437184 | bytes 14680072 | tf_op jit(solution)/shard_map/sub | solution.py:662
  (54 shorter events, 5.1 us)
Async XLA Ops:
  7.2 262.0 %all-reduce.2.cloned.1.call-start = ((), (), s32[]{:S(2)}) async-start(), calls=%async_computation | async-start | bytes 7421952 | tf_op jit(solution)/shard_map/psum | solution.py:701
  129.6 1.4 copy-start.4
  131.1 1.6 copy-start.13
  132.7 1.6 copy-start.14
  134.3 1.6 copy-start.22
  271.9 4.7 %copy-start = (f32[7248,256]{1,0:T(8,128)}, f32[7248,256]{1,0:T(8,128)S(1)}, u32[]{:S(2)}) copy-start(f32[7248,256]{1,0:T(8,128)S(1)} %convert_element_type.14) | copy-start | bytes 22265860
  319.2 3.1 copy-start.19
  319.2 3.1 copy-start.20
  319.2 3.1 copy-start.21
  322.2 6.1 %copy-start.6 = (f32[1,256,256]{2,1,0:T(8,128)S(1)}, f32[1,256,256]{2,1,0:T(8,128)}, u32[]{:S(2)}) copy-start(f32[1,256,256]{2,1,0:T(8,128)} %get-tuple-element.76) | copy-start | bytes 786436
  322.3 6.1 %copy-start.8 = (f32[2,256,256]{2,1,0:T(8,128)S(1)}, f32[2,256,256]{2,1,0:T(8,128)}, u32[]{:S(2)}) copy-start(f32[2,256,256]{2,1,0:T(8,128)} %attn_out_ref.1) | copy-start | bytes 1572868
  322.3 6.1 %copy-start.17 = (f32[2,256,256]{2,1,0:T(8,128)S(1)}, f32[2,256,256]{2,1,0:T(8,128)}, u32[]{:S(2)}) copy-start(f32[2,256,256]{2,1,0:T(8,128)} %param.42) | copy-start | bytes 1572868
  322.3 6.1 %copy-start.18 = (f32[2,256,256]{2,1,0:T(8,128)S(1)}, f32[2,256,256]{2,1,0:T(8,128)}, u32[]{:S(2)}) copy-start(f32[2,256,256]{2,1,0:T(8,128)} %param.43) | copy-start | bytes 1572868
  324.4 6.2 %copy-start.15 = (f32[256,533]{0,1:T(8,128)S(1)}, f32[256,533]{0,1:T(8,128)}, u32[]{:S(2)}) copy-start(f32[256,533]{0,1:T(8,128)} %param.54) | copy-start | bytes 1637380
  324.4 6.2 %copy-start.16 = (f32[256,533]{0,1:T(8,128)S(1)}, f32[256,533]{0,1:T(8,128)}, u32[]{:S(2)}) copy-start(f32[256,533]{0,1:T(8,128)} %param.55) | copy-start | bytes 1637380
  324.4 8.6 %copy-start.10 = (f32[2,1024,256]{2,1,0:T(8,128)S(1)}, f32[2,1024,256]{2,1,0:T(8,128)}, u32[]{:S(2)}) copy-start(f32[2,1024,256]{2,1,0:T(8,128)} %param.49) | copy-start | bytes 6291460
  328.4 2.3 copy-start.5
  328.4 2.3 copy-start.7
  328.4 4.6 %copy-start.9 = (f32[2,1024,256]{2,1,0:T(8,128)S(1)}, f32[2,1024,256]{2,1,0:T(8,128)}, u32[]{:S(2)}) copy-start(f32[2,1024,256]{2,1,0:T(8,128)} %param.48) | copy-start | bytes 6291460
  330.7 2.3 copy-start.1
  330.7 2.3 copy-start.2
  333.0 4.6 %copy-start.3 = (f32[2,256,1024]{2,1,0:T(8,128)S(1)}, f32[2,256,1024]{2,1,0:T(8,128)}, u32[]{:S(2)}) copy-start(f32[2,256,1024]{2,1,0:T(8,128)} %ffn_in_ref.1) | copy-start | bytes 6291460
  333.0 4.6 %copy-start.11 = (f32[2,256,1024]{2,1,0:T(8,128)S(1)}, f32[2,256,1024]{2,1,0:T(8,128)}, u32[]{:S(2)}) copy-start(f32[2,256,1024]{2,1,0:T(8,128)} %param.45) | copy-start | bytes 6291460
  333.0 4.5 %copy-start.12 = (f32[2,256,1024]{2,1,0:T(8,128)S(1)}, f32[2,256,1024]{2,1,0:T(8,128)}, u32[]{:S(2)}) copy-start(f32[2,256,1024]{2,1,0:T(8,128)} %param.46) | copy-start | bytes 6291460
Sparse Core Ops, SparseCore 0:
  129.8 139.3 all-reduce.1

commit v2 on v1

--- a/solution.py
+++ b/solution.py
@@ -3,6 +3,7 @@
 
 import jax
 import jax.numpy as jnp
+import numpy as np
 from jax import lax
 from jax.experimental import pallas as pl
 from jax.experimental.pallas import tpu as pltpu
@@ -27,7 +28,8 @@
 BF = jnp.bfloat16
 F32 = jnp.float32
 ROWS = 256
-WIN = 128
+QRY = 2 * SEG
+KEY = 3 * SEG
 OUTS = 544
 NEG = -1e30
 MESH = pl.DeviceIdType.MESH
@@ -73,7 +75,7 @@
     rewards_ref,
     continues_ref,
     values_ref,
-    freq_ref,
+    trig_ref,
     table_ref,
     attn_in_ref,
     attn_out_ref,
@@ -97,7 +99,7 @@
     acts,
     gds,
     mixes,
-    bias,
+    lows,
     tokf,
     toki,
     gouts,
@@ -109,7 +111,6 @@
     dgain,
     lossacc,
     lam,
-    ang,
     bsend,
     brecv,
     send_sem,
@@ -120,11 +121,12 @@
     dims = gains_ref.shape[1]
     ff = ffn_in_ref.shape[2]
     tiles = span // SEG
+    pairs = span // QRY
     total = batch * span
     chunks = total // ROWS
     per_seq = span // ROWS
     vocab_all = table_ref.shape[0]
-    outs_all = readout_ref.shape[1]
+    outs_all = readout_ref.shape[0]
     head_dim = dims // HEADS
     scale = head_dim ** (-0.5)
     exp_scale = scale * math.log2(math.e)
@@ -160,13 +162,8 @@
         block_copy(k).start()
     tb[...] = jnp.zeros_like(tb)
     tb[0:vocab_all, :] = table_ref[...].astype(BF)
-    for part in range(VOCAB // 256):
-        rt[part * 256 : part * 256 + 256, :] = readout_ref[:, part * 256 : part * 256 + 256].T.astype(BF)
-    rest = outs_all - VOCAB
-    tail = jnp.concatenate(
-        [readout_ref[:, VOCAB:outs_all], jnp.zeros((dims, 128 - rest), F32)], axis=1
-    ).T
-    rt[VOCAB:OUTS, :] = tail[0 : OUTS - VOCAB].astype(BF)
+    rt[...] = jnp.zeros_like(rt)
+    rt[0:outs_all, :] = readout_ref[...].astype(BF)
 
     ends = []
     for b in range(batch):
@@ -212,51 +209,49 @@
         toki[c, 2:3, :] = next_ref[b : b + 1, lanes]
 
     half = dims // 2
-    freq = freq_ref[...]
-    in_angle = iota((SEG, half), 0).astype(F32) * freq
-    in_sin, in_cos = jnp.sin(in_angle), jnp.cos(in_angle)
-    tile_angle = (iota((tiles, half), 0) * SEG + base).astype(F32) * freq
-    all_sin, all_cos = jnp.sin(tile_angle), jnp.cos(tile_angle)
-    for tile in range(tiles):
-        ang[tile, 0:1, :] = all_sin[tile : tile + 1, :]
-        ang[tile, 1:2, :] = all_cos[tile : tile + 1, :]
-    end_row = iota((batch * episodes, half), 0)
-    end_all = jnp.zeros((batch * episodes, half), jnp.int32)
+    in_sin, in_cos = trig_ref[0:SEG, 2, :], trig_ref[0:SEG, 3, :]
+    end_sin, end_cos = [], []
     for b in range(batch):
         for e in range(episodes):
-            end_all = jnp.where(end_row == b * episodes + e, ends[b][e], end_all)
-    end_angle = end_all.astype(F32) * freq
-    end_sin, end_cos = jnp.sin(end_angle), jnp.cos(end_angle)
+            far, near = lax.div(ends[b][e], SEG), lax.rem(ends[b][e], SEG)
+            far_sin, far_cos = trig_ref[far, 0:1, :], trig_ref[far, 1:2, :]
+            near_sin, near_cos = trig_ref[near, 2:3, :], trig_ref[near, 3:4, :]
+            end_sin.append(far_sin * near_cos + far_cos * near_sin)
+            end_cos.append(far_cos * near_cos - far_sin * near_sin)
 
     def marks(tile, carry):
-        tile_sin = ang[tile, 0:1, :]
-        tile_cos = ang[tile, 1:2, :]
+        at = me * tiles + tile
+        tile_sin, tile_cos = trig_ref[at, 0:1, :], trig_ref[at, 1:2, :]
         here_sin = in_sin * tile_cos + in_cos * tile_sin
         here_cos = in_cos * tile_cos - in_sin * tile_sin
         place = iota((SEG, half), 0) + (base + tile * SEG)
-        key_place = iota((SEG, WIN), 1) + (base + tile * SEG - SEG)
         for b in range(batch):
-            start = jnp.zeros((SEG, half), jnp.int32)
             start_sin = jnp.zeros((SEG, half), F32)
             start_cos = jnp.ones((SEG, half), F32)
             for e in range(episodes):
                 passed = place >= ends[b][e]
                 row = b * episodes + e
-                start = jnp.where(passed, ends[b][e], start)
-                start_sin = jnp.where(passed, end_sin[row : row + 1, :], start_sin)
-                start_cos = jnp.where(passed, end_cos[row : row + 1, :], start_cos)
+                start_sin = jnp.where(passed, end_sin[row], start_sin)
+                start_cos = jnp.where(passed, end_cos[row], start_cos)
             rows = pl.ds(pl.multiple_of(b * span + tile * SEG, SEG), SEG)
             xs[0, rows, 0:half] = here_sin * start_cos - here_cos * start_sin
             xs[0, rows, half:dims] = here_cos * start_cos + here_sin * start_sin
-            seen = (key_place <= place) & (key_place >= start)
-            bias[rows, :] = jnp.where(seen, 0.0, NEG)
         return carry
 
     lax.fori_loop(0, tiles, marks, 0)
 
-    for layer in range(layers):
+    def lowest(pair, carry):
+        within = lax.rem(iota((8, groups * QRY), 1), QRY)
+        first = base + pair * QRY - SEG
+        place = within + (base + pair * QRY)
         for b in range(batch):
-            kvs[layer, b, SEG + span :, :] = jnp.zeros((kvs.shape[2] - SEG - span, 2 * dims), BF)
+            low = jnp.where(within >= SEG, SEG, 0)
+            for e in range(episodes):
+                low = jnp.where(place >= ends[b][e], jnp.maximum(low, ends[b][e] - first), low)
+            lows[b * pairs + pair] = jnp.maximum(low, -first)
+        return carry
+
+    lax.fori_loop(0, pairs, lowest, 0)
 
     def chunk_rows(c):
         return pl.ds(pl.multiple_of(c * ROWS, ROWS), ROWS)
@@ -295,9 +290,9 @@
         return jnp.concatenate([keys * even_mask, keys * odd_mask], axis=0)
 
     def gather_heads(wide):
-        out = wide[0:SEG]
+        out = wide[0:QRY]
         for g in range(1, groups):
-            out = jnp.where(lane_head // 2 == g, wide[g * SEG : g * SEG + SEG], out)
+            out = jnp.where(lane_head // 2 == g, wide[g * QRY : g * QRY + QRY], out)
         return out
 
     def forward_copy(layer):
@@ -332,37 +327,43 @@
 
         lax.fori_loop(0, chunks, body, 0)
 
+    def pair_rows(b, pair):
+        return pl.ds(pl.multiple_of(b * span + pair * QRY, 16), QRY)
+
+    def pair_window(pair):
+        return pl.ds(pl.multiple_of(pair * QRY, 16), KEY)
+
+    causal = iota((KEY, groups * QRY), 0) <= lax.rem(iota((KEY, groups * QRY), 1), QRY) + SEG
+    key_place = iota((KEY, groups * QRY), 0)
+
     def attend(layer):
-        def one(b, tile):
-            rows = pl.ds(pl.multiple_of(b * span + tile * SEG, SEG), SEG)
-            window = pl.ds(pl.multiple_of(tile * SEG, SEG), WIN)
+        def one(b, pair):
+            rows, window = pair_rows(b, pair), pair_window(pair)
             keys = kvs[layer, b, window, 0:dims]
             values = kvs[layer, b, window, dims:]
-            mask = bias[rows, :]
-            mask = jnp.concatenate([mask] * groups, axis=0)
-            scores = dot_nt(spread(qs[layer, rows, :]), both(keys))
+            seen = causal & (key_place >= lows[b * pairs + pair, 0:1, :])
+            scores = dot_nt(both(keys), spread(qs[layer, rows, :]))
             sides = []
             for side in range(2):
-                s = scores[:, side * WIN : side * WIN + WIN] + mask
-                top = jnp.max(s, axis=-1, keepdims=True)
+                s = jnp.where(seen, scores[side * KEY : side * KEY + KEY], NEG)
+                top = jnp.max(s, axis=0, keepdims=True)
                 e = jnp.exp2((s - top) * exp_scale)
-                sides.append((e / jnp.sum(e, axis=-1, keepdims=True)).astype(BF))
-            p = jnp.concatenate(sides, axis=1)
-            probs[layer, b * tiles + tile] = p
-            wide = dot_nn(p, both(values))
+                sides.append((e * (1.0 / jnp.sum(e, axis=0, keepdims=True))).astype(BF))
+            p = jnp.concatenate(sides, axis=0)
+            probs[layer, b * pairs + pair] = p
+            wide = dot_tn(p, both(values))
             mixes[layer, rows, :] = gather_heads(wide).astype(BF)
 
         def body(i, carry):
-            tile = tiles - 1 - i
             for b in range(batch):
-                one(b, tile)
+                one(b, pairs - 1 - i)
             return carry
 
         copy = forward_copy(layer)
         copy.start()
-        lax.fori_loop(0, tiles - 1, body, 0)
+        lax.fori_loop(0, pairs - 1, body, 0)
         copy.wait()
-        lax.fori_loop(tiles - 1, tiles, body, 0)
+        lax.fori_loop(pairs - 1, pairs, body, 0)
 
     def feed(layer):
         def body(c, carry):
@@ -394,6 +395,11 @@
     lossacc[...] = jnp.zeros_like(lossacc)
     dgain[...] = jnp.zeros_like(dgain)
     top_gain = gains_ref[2 * layers : 2 * layers + 1, :]
+
+    def put(at, block):
+        for side in range(2):
+            cols = slice(side * 128, side * 128 + 128)
+            grads_ref[side, at : at + block.shape[0], :] = block[:, cols].astype(BF)
 
     def losses(c, carry):
         rows = chunk_rows(c)
@@ -449,7 +455,9 @@
         return carry
 
     lax.fori_loop(0, chunks, losses, 0)
-    grads_ref[0:OUTS, :] = dot_nn(gouts[...], hs[2 * layers]).astype(BF)
+    tail_at = VOCAB + layers * 12 * 256 + OUTS
+    put(0, dot_nn(gouts[0:VOCAB, :], hs[2 * layers]))
+    put(tail_at, dot_nn(gouts[VOCAB:OUTS, :], hs[2 * layers]))
     loss_total = jnp.sum(lossacc[0:1, :])
     count_total = jnp.sum(lossacc[1:2, :])
     place = iota(scal_ref.shape, 0)
@@ -477,38 +485,37 @@
         lax.fori_loop(0, chunks, body, 0)
 
     def attend_back(layer):
-        def one(b, tile):
-            rows = pl.ds(pl.multiple_of(b * span + tile * SEG, SEG), SEG)
-            window = pl.ds(pl.multiple_of(tile * SEG, SEG), WIN)
+        def one(b, pair):
+            rows, window = pair_rows(b, pair), pair_window(pair)
             keys = both(kvs[layer, b, window, 0:dims])
             values = both(kvs[layer, b, window, dims:])
             queries = spread(qs[layer, rows, :])
             dout = spread(dmix[rows, :])
-            p = probs[layer, b * tiles + tile]
-            dp = dot_nt(dout, values)
+            p = probs[layer, b * pairs + pair]
+            dp = dot_nt(values, dout)
             sides = []
             for side in range(2):
-                cols = slice(side * WIN, side * WIN + WIN)
-                pf = p[:, cols].astype(F32)
-                d = dp[:, cols]
-                sides.append((pf * (d - jnp.sum(d * pf, axis=-1, keepdims=True))).astype(BF))
-            ds = jnp.concatenate(sides, axis=1)
-            dq = gather_heads(dot_nn(ds, keys)) * scale
+                part = slice(side * KEY, side * KEY + KEY)
+                pf = p[part].astype(F32)
+                d = dp[part]
+                sides.append((pf * (d - jnp.sum(d * pf, axis=0, keepdims=True))).astype(BF))
+            ds = jnp.concatenate(sides, axis=0)
+            dq = gather_heads(dot_tn(ds, keys)) * scale
             dqkv[rows, 0:dims] = dq.astype(BF)
-            dk = dot_tn(ds, queries) * scale
-            dk = jnp.where(even_f, dk[0 : 2 * SEG], dk[WIN : WIN + 2 * SEG])
-            dv = dot_tn(p, dout)
-            dv = jnp.where(even_f, dv[0 : 2 * SEG], dv[WIN : WIN + 2 * SEG])
-            old = pl.ds(pl.multiple_of(tile * SEG, SEG), SEG)
-            new = pl.ds(pl.multiple_of(tile * SEG + SEG, SEG), SEG)
+            dk = dot_nn(ds, queries) * scale
+            dk = jnp.where(even_f, dk[0:KEY], dk[KEY:])
+            dv = dot_nn(p, dout)
+            dv = jnp.where(even_f, dv[0:KEY], dv[KEY:])
+            old = pl.ds(pl.multiple_of(pair * QRY, 16), SEG)
+            new = pl.ds(pl.multiple_of(pair * QRY + SEG, 16), QRY)
             dkv[b, old, 0:dims] += dk[0:SEG]
             dkv[b, old, dims:] += dv[0:SEG]
             dkv[b, new, 0:dims] = dk[SEG:]
             dkv[b, new, dims:] = dv[SEG:]
 
-        def body(tile, carry):
+        def body(pair, carry):
             for b in range(batch):
-                one(b, tile)
+                one(b, pair)
             return carry
 
         for b in range(batch):
@@ -518,7 +525,7 @@
             bsend[layer, b] = dkv[b, 0:SEG, :].astype(BF)
         copy = backward_copy(layer)
         copy.start()
-        lax.fori_loop(1, tiles, body, 0)
+        lax.fori_loop(1, pairs, body, 0)
         copy.wait()
         for b in range(batch):
             dkv[b, span : span + SEG, :] += brecv[layer, b].astype(F32)
@@ -536,25 +543,25 @@
 
         lax.fori_loop(0, chunks, body, 0)
 
-    at = OUTS
+    at = VOCAB
     for layer in reversed(range(layers)):
         feed_back(layer)
         for j in range(ff // 256):
             cols = slice(j * 256, j * 256 + 256)
-            grads_ref[at : at + 256, :] = dot_tn(acts[layer, :, cols], gl[...]).astype(BF)
+            put(at, dot_tn(acts[layer, :, cols], gl[...]))
             at += 256
         for j in range(ff // 256):
             cols = slice(j * 256, j * 256 + 256)
-            grads_ref[at : at + 256, :] = dot_tn(hs[2 * layer + 1], gds[layer, :, cols]).astype(BF)
+            put(at, dot_tn(hs[2 * layer + 1], gds[layer, :, cols]))
             at += 256
         gl[...] = gx[...].astype(BF)
-        grads_ref[at : at + 256, :] = dot_tn(mixes[layer], gl[...]).astype(BF)
+        put(at, dot_tn(mixes[layer], gl[...]))
         at += 256
         attend_back(layer)
         project_back(layer)
         for j in range(3):
             cols = slice(j * 256, j * 256 + 256)
-            grads_ref[at : at + 256, :] = dot_tn(hs[2 * layer], dqkv[:, cols]).astype(BF)
+            put(at, dot_tn(hs[2 * layer], dqkv[:, cols]))
             at += 256
     gl[...] = gx[...].astype(BF)
 
@@ -563,13 +570,15 @@
         return carry
 
     lax.fori_loop(0, chunks, mark, 0)
-    grads_ref[at : at + OUTS, :] = dot_nn(gouts[...], gl[...]).astype(BF)
-    at += OUTS
+    put(at, dot_nn(gouts[...], gl[...]))
+    at = tail_at + OUTS - VOCAB
     place = iota((16, dims), 0)
     gain_rows = jnp.zeros((16, dims), F32)
     for index in range(2 * layers + 1):
         gain_rows = jnp.where(place == index, jnp.sum(dgain[index], axis=0, keepdims=True), gain_rows)
-    grads_ref[at : at + 16, :] = gain_rows.astype(BF)
+    put(at, gain_rows)
+    at += 16
+    put(at, jnp.zeros((grads_ref.shape[1] - at, dims), F32))
 
 
 def gradients(codes, actions, next_codes, lengths, rewards, continues, values, weights, seq_size):
@@ -579,20 +588,22 @@
     total = batch * span
     tiles = span // SEG
     chunks = total // ROWS
-    grad_rows = 2 * OUTS + layers * 12 * 256 + 16
-    freq = jnp.exp(
-        jnp.arange(dims // 2).astype(F32) * (-2.0 * math.log(10000.0) / dims)
-    )[None, :]
+    grad_rows = grad_row_count(layers)
+    steps = np.arange(lax.axis_size("seq") * tiles + 1, dtype=np.float64)[:, None]
+    freq = np.exp(np.arange(dims // 2) * (-2.0 * math.log(10000.0) / dims))
+    trig = np.zeros((steps.shape[0], 8, dims // 2), np.float32)
+    trig[:, 0], trig[:, 1] = np.sin(steps * SEG * freq), np.cos(steps * SEG * freq)
+    trig[:, 2], trig[:, 3] = np.sin(steps * freq), np.cos(steps * freq)
+    trig = jnp.asarray(trig)
     vmem = pl.BlockSpec(memory_space=pltpu.VMEM)
     smem = pl.BlockSpec(memory_space=pltpu.SMEM)
-    kv_span = -(-(span - SEG + WIN) // 16) * 16
     return pl.pallas_call(
         functools.partial(step_kernel, layers, seq_size),
         out_shape=(
-            jax.ShapeDtypeStruct((grad_rows, dims), BF),
+            jax.ShapeDtypeStruct((2, grad_rows, dims // 2), BF),
             jax.ShapeDtypeStruct((8, 128), F32),
         ),
-        in_specs=[vmem] * 3 + [smem] + [vmem] * 5 + [pl.BlockSpec(memory_space=pl.ANY)] * 4 + [vmem] * 2,
+        in_specs=[vmem] * 3 + [smem] + [vmem] * 5 + [pl.BlockSpec(memory_space=pltpu.HBM)] * 4 + [vmem] * 2,
         out_specs=(vmem, vmem),
         scratch_shapes=[
             pltpu.VMEM((layers, dims, 3 * dims), BF),
@@ -604,12 +615,12 @@
             pltpu.VMEM((2 * layers + 1, total, dims), F32),
             pltpu.VMEM((2 * layers + 1, total, dims), BF),
             pltpu.VMEM((layers, total, dims), BF),
-            pltpu.VMEM((layers, batch, kv_span, 2 * dims), BF),
-            pltpu.VMEM((layers, batch * tiles, HEADS // 2 * SEG, 2 * WIN), BF),
+            pltpu.VMEM((layers, batch, SEG + span, 2 * dims), BF),
+            pltpu.VMEM((layers, total // QRY, 2 * KEY, HEADS // 2 * QRY), BF),
             pltpu.VMEM((layers, total, ff), BF),
             pltpu.VMEM((layers, total, ff), BF),
             pltpu.VMEM((layers, total, dims), BF),
-            pltpu.VMEM((total, WIN), F32),
+            pltpu.VMEM((total // QRY, 8, HEADS // 2 * QRY), jnp.int32),
             pltpu.VMEM((chunks, 8, ROWS), F32),
             pltpu.VMEM((chunks, 8, ROWS), jnp.int32),
             pltpu.VMEM((OUTS, total), BF),
@@ -621,7 +632,6 @@
             pltpu.VMEM((2 * layers + 1, 8, dims), F32),
             pltpu.VMEM((8, ROWS), F32),
             pltpu.VMEM((4, 8, span), F32),
-            pltpu.VMEM((tiles, 8, dims // 2), F32),
             pltpu.VMEM((layers, batch, SEG, 2 * dims), BF),
             pltpu.VMEM((layers, batch, SEG, 2 * dims), BF),
             pltpu.SemaphoreType.DMA((2 * layers,)),
@@ -640,7 +650,7 @@
         rewards,
         continues,
         values,
-        freq,
+        trig,
         table,
         attn_in,
         attn_out,
@@ -649,6 +659,328 @@
         gains,
         readout,
     )
+
+
+def grad_row_count(layers):
+    rows = VOCAB + layers * 12 * 256 + OUTS + (OUTS - VOCAB) + 16
+    return -(-rows // 256) * 256
+
+
+def buckets_of(layers):
+    cuts = [0, VOCAB + 8 * 256]
+    for layer in range(layers):
+        cuts.append(cuts[-1] + 4 * 256)
+        if layer < layers - 1:
+            cuts.append(cuts[-1] + 8 * 256)
+    cuts[-1] = grad_row_count(layers)
+    return list(zip(cuts[:-1], cuts[1:]))
+
+
+class Exchange:
+    def __init__(self, seq_size, dp_size, source, total, core_in, seq_in, deep_in, sems):
+        self.seq_size, self.deep = seq_size, dp_size // 2
+        self.owners = min(4, self.deep)
+        self.source, self.total = source, total
+        self.core_in, self.seq_in, self.deep_in = core_in, seq_in, deep_in
+        self.send_sem, self.recv_sem = sems
+        self.at_seq = lax.axis_index("seq")
+        at_dp = lax.axis_index("dp")
+        self.core = lax.rem(at_dp, 2)
+        self.at_deep = lax.div(at_dp, 2)
+
+    def sibling(self):
+        return {"dp": self.at_deep * 2 + 1 - self.core}
+
+    def seq_peer(self, k):
+        return {"seq": lax.rem(self.at_seq + k, self.seq_size)}
+
+    def deep_peer(self, k):
+        return {"dp": lax.rem(self.at_deep + k, self.deep) * 2 + self.core}
+
+    def peers(self):
+        found = [self.sibling()]
+        found += [self.seq_peer(k) for k in range(1, self.seq_size)]
+        return found + [self.deep_peer(k) for k in range(1, self.deep)]
+
+    def greet(self):
+        barrier = pltpu.get_barrier_semaphore()
+        found = self.peers()
+        for peer in found:
+            pl.semaphore_signal(barrier, inc=1, device_id=peer, device_id_type=MESH)
+        pl.semaphore_wait(barrier, len(found))
+
+    def copy(self, src, dst, bucket, slot, peer):
+        return pltpu.make_async_remote_copy(
+            src_ref=src,
+            dst_ref=dst,
+            send_sem=self.send_sem.at[bucket, slot],
+            recv_sem=self.recv_sem.at[bucket, slot],
+            device_id=peer,
+            device_id_type=MESH,
+        )
+
+    def only(self, condition, act):
+        if self.owners == self.deep:
+            act()
+        else:
+            pl.when(condition)(act)
+
+    def slots(self):
+        return 2 * (1 + self.seq_size - 1 + self.deep - 1)
+
+    def parts(self, bucket):
+        r0, r1 = bucket
+        quarter = (r1 - r0) // self.seq_size
+        return r0, r1 - r0, quarter, quarter // self.owners
+
+    def seq_rows(self, bucket, index):
+        r0, _, quarter, _ = self.parts(bucket)
+        return pl.ds(pl.multiple_of(r0 + index * quarter, 16), quarter)
+
+    def share_rows(self, bucket, index):
+        r0, _, quarter, share = self.parts(bucket)
+        return pl.ds(pl.multiple_of(r0 // self.seq_size + index * share, 16), share)
+
+    def own_rows(self, bucket):
+        r0, _, quarter, share = self.parts(bucket)
+        at = r0 + self.at_seq * quarter + lax.rem(self.at_deep, self.owners) * share
+        return pl.ds(pl.multiple_of(at, 16), share)
+
+    def core_copy(self, n, bucket):
+        r0, rows, _, _ = self.parts(bucket)
+        part = pl.ds(r0, rows)
+        return self.copy(self.source.at[1 - self.core, part], self.core_in.at[part], n, 0, self.sibling())
+
+    def seq_copies(self, n, bucket):
+        r0, _, quarter, _ = self.parts(bucket)
+        found = []
+        for k in range(1, self.seq_size):
+            rows = self.seq_rows(bucket, lax.rem(self.at_seq + k, self.seq_size))
+            dest = self.seq_in.at[k - 1, pl.ds(r0 // self.seq_size, quarter)]
+            found.append(self.copy(self.core_in.at[rows], dest, n, k, self.seq_peer(k)))
+        return found
+
+    def deep_copy(self, n, bucket, k):
+        r0, _, _, share = self.parts(bucket)
+        target = lax.rem(self.at_deep + k, self.deep)
+        rows = self.share_rows(bucket, lax.rem(target, self.owners))
+        dest = self.deep_in.at[k - 1, pl.ds(r0 // (self.seq_size * self.owners), share)]
+        return self.copy(self.seq_out.at[rows], dest, n, self.seq_size - 1 + k, self.deep_peer(k))
+
+    def back_copy(self, n, rows, slot, peer):
+        there = self.total.at[self.core, rows]
+        return self.copy(there, there, n, self.slots() // 2 + slot, peer)
+
+    def core_start(self, n, bucket):
+        self.core_copy(n, bucket).start()
+
+    def core_finish(self, n, bucket):
+        self.core_copy(n, bucket).wait()
+        r0, rows, _, _ = self.parts(bucket)
+
+        def add(i, carry):
+            part = pl.ds(pl.multiple_of(r0 + i * 256, 256), 256)
+            both = self.source[self.core, part, :].astype(F32) + self.core_in[part, :].astype(F32)
+            self.core_in[part, :] = both.astype(BF)
+            return carry
+
+        lax.fori_loop(0, rows // 256, add, 0)
+
+    def seq_start(self, n, bucket):
+        for copy in self.seq_copies(n, bucket):
+            copy.start()
+
+    def seq_finish(self, n, bucket):
+        for copy in self.seq_copies(n, bucket):
+            copy.wait()
+        r0, _, quarter, _ = self.parts(bucket)
+
+        def add(i, carry):
+            here = pl.ds(pl.multiple_of(r0 + self.at_seq * quarter + i * 64, 16), 64)
+            part = pl.ds(pl.multiple_of(r0 // self.seq_size + i * 64, 16), 64)
+            both = self.core_in[here, :].astype(F32)
+            for k in range(self.seq_size - 1):
+                both = both + self.seq_in[k, part, :].astype(F32)
+            self.seq_out[part, :] = both.astype(BF)
+            return carry
+
+        lax.fori_loop(0, quarter // 64, add, 0)
+
+    def deep_start(self, n, bucket):
+        for k in range(1, self.deep):
+            target = lax.rem(self.at_deep + k, self.deep)
+            self.only(target < self.owners, self.deep_copy(n, bucket, k).start)
+
+    def deep_finish(self, n, bucket):
+        r0, _, _, share = self.parts(bucket)
+        for k in range(1, self.deep):
+            target = lax.rem(self.at_deep + k, self.deep)
+            self.only(target < self.owners, self.deep_copy(n, bucket, k).wait_send)
+
+        def act():
+            for k in range(1, self.deep):
+                self.deep_copy(n, bucket, k).wait_recv()
+            mine = self.share_rows(bucket, lax.rem(self.at_deep, self.owners))
+            both = self.seq_out[mine, :].astype(F32)
+            part = pl.ds(r0 // (self.seq_size * self.owners), share)
+            for k in range(self.deep - 1):
+                both = both + self.deep_in[k, part, :].astype(F32)
+            self.total[self.core, self.own_rows(bucket), :] = both.astype(BF)
+            squares = (both * both).reshape(share // 8, 8, both.shape[1])
+            self.squares[...] += jnp.sum(squares, axis=0)
+
+        self.only(self.at_deep < self.owners, act)
+
+    def back_deep(self, n, bucket, k):
+        return self.back_copy(n, self.own_rows(bucket), self.seq_size - 1 + k, self.deep_peer(k))
+
+    def back_deep_start(self, n, bucket):
+        def act():
+            for k in range(1, self.deep):
+                self.back_deep(n, bucket, k).start()
+
+        self.only(self.at_deep < self.owners, act)
+
+    def back_deep_finish(self, n, bucket):
+        def act():
+            for k in range(1, self.deep):
+                self.back_deep(n, bucket, k).wait_send()
+
+        self.only(self.at_deep < self.owners, act)
+        for k in range(1, self.deep):
+            origin = lax.rem(self.at_deep + self.deep - k, self.deep)
+            self.only(origin < self.owners, self.back_deep(n, bucket, k).wait_recv)
+
+    def back_seq(self, n, bucket):
+        rows = self.seq_rows(bucket, self.at_seq)
+        return [self.back_copy(n, rows, k, self.seq_peer(k)) for k in range(1, self.seq_size)]
+
+    def back_seq_start(self, n, bucket):
+        for copy in self.back_seq(n, bucket):
+            copy.start()
+
+    def back_seq_finish(self, n, bucket):
+        for copy in self.back_seq(n, bucket):
+            copy.wait()
+
+    def back_core(self, n, bucket):
+        r0, rows, _, _ = self.parts(bucket)
+        return self.back_copy(n, pl.ds(r0, rows), 0, self.sibling())
+
+    def back_core_start(self, n, bucket):
+        self.back_core(n, bucket).start()
+
+    def back_core_finish(self, n, bucket):
+        self.back_core(n, bucket).wait()
+
+    def tile_copies(self, n, tile, phase):
+        if phase == 0:
+            slots, peers = [0], [self.sibling()]
+        elif phase == 1:
+            slots = list(range(1, self.seq_size))
+            peers = [self.seq_peer(k) for k in slots]
+        else:
+            slots = [self.seq_size - 1 + k for k in range(1, self.deep)]
+            peers = [self.deep_peer(k) for k in range(1, self.deep)]
+        return [
+            self.copy(self.tile_out.at[tile, phase], self.tile_in.at[tile, slot], n, slot, peer)
+            for slot, peer in zip(slots, peers)
+        ], slots
+
+    def tile_start(self, n, tile, phase):
+        for copy in self.tile_copies(n, tile, phase)[0]:
+            copy.start()
+
+    def tile_finish(self, n, tile, phase):
+        copies, slots = self.tile_copies(n, tile, phase)
+        for copy in copies:
+            copy.wait()
+        both = self.tile_out[tile, phase]
+        for slot in slots:
+            both = both + self.tile_in[tile, slot]
+        self.tile_out[tile, phase + 1] = both
+
+
+def sum_kernel(sizes, buckets, source, scal_ref, total, out_ref, core_in, seq_in, seq_out, deep_in,
+               squares, tile_out, tile_in, send_sem, recv_sem):
+    ex = Exchange(*sizes, source, total, core_in, seq_in, deep_in, (send_sem, recv_sem))
+    ex.seq_out, ex.squares, ex.tile_out, ex.tile_in = seq_out, squares, tile_out, tile_in
+    ex.greet()
+    squares[...] = jnp.zeros_like(squares)
+    listed = list(enumerate(buckets))
+    first, second = len(buckets), len(buckets) + 1
+    tile_out[0, 0] = scal_ref[...]
+    for n, bucket in listed:
+        ex.core_start(n, bucket)
+    ex.tile_start(first, 0, 0)
+    for n, bucket in listed:
+        ex.core_finish(n, bucket)
+        ex.seq_start(n, bucket)
+    ex.tile_finish(first, 0, 0)
+    ex.tile_start(first, 0, 1)
+    for n, bucket in listed:
+        ex.seq_finish(n, bucket)
+        ex.deep_start(n, bucket)
+    ex.tile_finish(first, 0, 1)
+    ex.tile_start(first, 0, 2)
+    for n, bucket in listed:
+        ex.deep_finish(n, bucket)
+        ex.back_deep_start(n, bucket)
+    ex.tile_finish(first, 0, 2)
+    tile_out[1, 0] = squares[...]
+    ex.tile_start(second, 1, 0)
+    for n, bucket in listed:
+        ex.back_deep_finish(n, bucket)
+        ex.back_seq_start(n, bucket)
+    ex.tile_finish(second, 1, 0)
+    ex.tile_start(second, 1, 1)
+    for n, bucket in listed:
+        ex.back_seq_finish(n, bucket)
+        ex.back_core_start(n, bucket)
+    ex.tile_finish(second, 1, 1)
+    ex.tile_start(second, 1, 2)
+    ex.tile_finish(second, 1, 2)
+    for n, bucket in listed:
+        ex.back_core_finish(n, bucket)
+    count = tile_out[0, 3, 1:2, 0:1]
+    average = jnp.sum(tile_out[1, 3]) / (count * count)
+    norm = jnp.sqrt(average)
+    place = iota(out_ref.shape, 0)
+    out = jnp.where(place == 2, norm, tile_out[0, 3])
+    out_ref[...] = jnp.where(place == 3, jnp.minimum(1.0, CLIP_NORM / norm) / count, out)
+
+
+def sum_gradients(grads, scal, layers, seq_size, dp_size):
+    buckets = buckets_of(layers)
+    rows = grads.shape[1]
+    deep = dp_size // 2
+    owners = min(4, deep)
+    slots = 2 * (seq_size + deep - 1)
+    vmem = pl.BlockSpec(memory_space=pltpu.VMEM)
+    return pl.pallas_call(
+        functools.partial(sum_kernel, (seq_size, dp_size), buckets),
+        out_shape=(
+            jax.ShapeDtypeStruct(grads.shape, BF),
+            jax.ShapeDtypeStruct((8, 128), F32),
+        ),
+        in_specs=[vmem, vmem],
+        out_specs=(vmem, vmem),
+        scratch_shapes=[
+            pltpu.VMEM((rows, 128), BF),
+            pltpu.VMEM((seq_size - 1, rows // seq_size, 128), BF),
+            pltpu.VMEM((rows // seq_size, 128), BF),
+            pltpu.VMEM((deep - 1, rows // (seq_size * owners), 128), BF),
+            pltpu.VMEM((8, 128), F32),
+            pltpu.VMEM((2, 4, 8, 128), F32),
+            pltpu.VMEM((2, slots // 2, 8, 128), F32),
+            pltpu.SemaphoreType.DMA((len(buckets) + 2, slots)),
+            pltpu.SemaphoreType.DMA((len(buckets) + 2, slots)),
+        ],
+        compiler_params=pltpu.CompilerParams(
+            collective_id=1, has_side_effects=True, vmem_limit_bytes=62 * 1024 * 1024
+        ),
+        name="sum_gradients",
+    )(grads, scal)
 
 
 def adam_update(weight, first_mom, second_mom, clipped, rate):
@@ -662,56 +994,141 @@
     return (weight - rate * (ratio + DECAY * weight), new_first, new_second)
 
 
-def unpack(grads, weights):
-    table, attn_in, attn_out, ffn_in, ffn_out, gains, readout = weights
-    layers, dims, ff = ffn_in.shape
-    read = grads[0:OUTS].T[:, : readout.shape[1]]
-    at = OUTS
-    per_layer = [None] * layers
+def update_kernel(layers, scal_ref, grads_ref, *refs):
+    ins, outs, here = refs[0:21], refs[21:42], refs[42:63]
+    load_sem, store_sem = refs[63], refs[64]
+    scale = scal_ref[3, 0]
+    pieces = [(slot, layer) for slot in (4, 3, 1, 2) for layer in range(layers)]
+    pieces += [(0, None), (6, None), (5, None)]
+
+    def view(ref, layer):
+        return ref if layer is None else ref.at[layer]
+
+    def moves(n, kind):
+        slot, layer = pieces[n]
+        for part in range(3):
+            index = 3 * slot + part
+            inside = view(here[index], layer)
+            if kind == 0:
+                yield pltpu.make_async_copy(view(ins[index], layer), inside, load_sem.at[n, part])
+            else:
+                yield pltpu.make_async_copy(inside, view(outs[index], layer), store_sem.at[n, part])
+
+    for n in range(len(pieces)):
+        for move in moves(n, 0):
+            move.start()
+
+    def renew(slot, layer, rows, cols, grad):
+        refs = [view(here[3 * slot + part], layer) for part in range(3)]
+        new = adam_update(*[ref[rows, cols] for ref in refs], grad.astype(F32) * scale, RATES[slot])
+        for ref, value in zip(refs, new):
+            ref[rows, cols] = value
+
+    offset = VOCAB
+    starts = {}
     for layer in reversed(range(layers)):
-        down = grads[at : at + ff]
-        at += ff
-        up = grads[at : at + ff].reshape(ff // 256, dims, 256).transpose(1, 0, 2).reshape(dims, ff)
-        at += ff
-        out = grads[at : at + dims]
-        at += dims
-        qkv = grads[at : at + 3 * dims].reshape(3, dims, 256).transpose(1, 0, 2).reshape(dims, 3 * dims)
-        at += 3 * dims
-        per_layer[layer] = (qkv, out, up, down)
-    tab = grads[at : at + table.shape[0]]
-    at += OUTS
-    gain = grads[at : at + gains.shape[0]]
-    stacked = [jnp.stack([entry[k] for entry in per_layer]) for k in range(4)]
-    return (tab, *stacked, gain, read)
+        starts[4, layer] = offset
+        starts[3, layer] = offset + 4 * 256
+        starts[2, layer] = offset + 8 * 256
+        starts[1, layer] = offset + 9 * 256
+        offset += 12 * 256
+    table_at, tail_at = offset, offset + OUTS
+    gains_at = tail_at + OUTS - VOCAB
+
+    for n, (slot, layer) in enumerate(pieces):
+        for move in moves(n, 0):
+            move.wait()
+        if layer is not None:
+            rows_all, cols_all = here[3 * slot].shape[1:]
+            at = starts[slot, layer]
+            for j in range(rows_all // 256):
+                for i in range(cols_all // 256):
+                    for side in range(2):
+                        cols = slice(i * 256 + side * 128, i * 256 + side * 128 + 128)
+
+                        def body(k, carry):
+                            rows = pl.ds(pl.multiple_of(j * 256 + k * 64, 64), 64)
+                            block = at + (j + i) * 256 + k * 64
+                            grad = grads_ref[side, pl.ds(pl.multiple_of(block, 64), 64), :]
+                            renew(slot, layer, rows, cols, grad)
+                            return carry
+
+                        lax.fori_loop(0, 4, body, 0)
+        elif slot == 0:
+            rows_all = here[0].shape[0]
+            for side in range(2):
+                cols = slice(side * 128, side * 128 + 128)
+
+                def body(k, carry):
+                    rows = pl.ds(pl.multiple_of(k * 64, 64), 64)
+                    block = pl.ds(pl.multiple_of(table_at + k * 64, 64), 64)
+                    renew(0, None, rows, cols, grads_ref[side, block, :])
+                    return carry
+
+                full = rows_all // 64
+                lax.fori_loop(0, full, body, 0)
+                if rows_all % 64:
+                    last = slice(full * 64, rows_all)
+                    block = grads_ref[side, table_at + full * 64 : table_at + full * 64 + 64, :]
+                    renew(0, None, last, cols, block.astype(F32)[0 : rows_all % 64])
+        elif slot == 6:
+            outs_all = here[18].shape[0]
+            for side in range(2):
+                cols = slice(side * 128, side * 128 + 128)
+
+                def body(k, carry):
+                    rows = pl.ds(pl.multiple_of(k * 64, 64), 64)
+                    renew(6, None, rows, cols, grads_ref[side, rows, :])
+                    return carry
+
+                lax.fori_loop(0, VOCAB // 64, body, 0)
+                rest = grads_ref[side, tail_at : tail_at + OUTS - VOCAB, :].astype(F32)
+                renew(6, None, slice(VOCAB, outs_all), cols, rest[0 : outs_all - VOCAB])
+        else:
+            count = here[15].shape[0]
+            for side in range(2):
+                cols = slice(side * 128, side * 128 + 128)
+                grad = grads_ref[side, gains_at : gains_at + 16, :].astype(F32)[0:count]
+                renew(5, None, slice(0, count), cols, grad)
+        for move in moves(n, 1):
+            move.start()
+    for n in range(len(pieces)):
+        for move in moves(n, 1):
+            move.wait()
+
+
+def update(grads, scal, state):
+    layers = state[3].shape[0]
+    anywhere = pl.BlockSpec(memory_space=pltpu.HBM)
+    pieces = 4 * layers + 3
+    return pl.pallas_call(
+        functools.partial(update_kernel, layers),
+        out_shape=tuple(jax.ShapeDtypeStruct(x.shape, F32) for x in state),
+        in_specs=[
+            pl.BlockSpec(memory_space=pltpu.SMEM),
+            pl.BlockSpec(memory_space=pltpu.VMEM),
+        ]
+        + [anywhere] * 21,
+        out_specs=(anywhere,) * 21,
+        scratch_shapes=[pltpu.VMEM(x.shape, F32) for x in state]
+        + [pltpu.SemaphoreType.DMA((pieces, 3)), pltpu.SemaphoreType.DMA((pieces, 3))],
+        compiler_params=pltpu.CompilerParams(vmem_limit_bytes=62 * 1024 * 1024),
+        name="update",
+    )(scal, grads, *state)
 
 
 def local(codes, actions, next_codes, lengths, rewards, continues, target_values, *state):
-    params, firsts, seconds = state[0::3], state[1::3], state[2::3]
+    state = state[0:18] + tuple(value.T for value in state[18:21])
+    params = state[0::3]
+    seq_size, dp_size = lax.axis_size("seq"), lax.axis_size("dp")
+    layers = params[1].shape[0]
     grads, scal = gradients(
-        codes,
-        actions,
-        next_codes,
-        lengths,
-        rewards,
-        continues,
-        target_values,
-        params,
-        lax.axis_size("seq"),
+        codes, actions, next_codes, lengths, rewards, continues, target_values, params, seq_size
     )
-    grads = lax.psum(grads, ("seq", "dp")).astype(F32)
-    scal = lax.psum(scal, ("seq", "dp"))
-    loss_sum, step_count = scal[0, 0], scal[1, 0]
-    averaged = [grad / step_count for grad in unpack(grads, params)]
-    grad_norm = jnp.sqrt(sum((jnp.sum(grad * grad) for grad in averaged)))
-    factor = jnp.minimum(1.0, CLIP_NORM / grad_norm)
-    results = []
-    for slot in range(7):
-        results.extend(
-            adam_update(
-                params[slot], firsts[slot], seconds[slot], averaged[slot] * factor, RATES[slot]
-            )
-        )
-    return tuple(results) + (loss_sum, step_count, grad_norm)
+    grads, scal = sum_gradients(grads, scal, layers, seq_size, dp_size)
+    results = list(update(grads, scal, state))
+    results[18:21] = [value.T for value in results[18:21]]
+    return tuple(results) + (scal[0, 0], scal[1, 0], scal[2, 0])
 
 
 def solution(mesh):

time: 351 us -> 181 us (0.52)
  waiting for transfers between devices: 93.2 us -> 0 us
  Pallas kernels: 120 us -> 179 us
  other arithmetic: 45 us -> 0 us
  blocking collectives: 39.6 us -> 0 us
  local copies, waits for them, and re-layouts: 32.5 us -> 1.32 us
  between operations: 20 us -> 0.69 us
    psum x1 -> x0, waiting for transfers between devices: 93.2 us -> none  [local(): grads = lax.psum(grads, ('seq', 'dp')).astype(F32)]
    pallas_call x0 -> x2, Pallas kernels: none -> 86.8 us  [the longest x1 69.4 us: sum_gradients(): pl.pallas_call(functools.partial(sum_kernel, (seq_size, dp_size), buckets...]
    psum x1 -> x0, blocking collectives: 39.6 us -> none  [local(): scal = lax.psum(scal, ('seq', 'dp'))]
    pallas_call x1, Pallas kernels: 120 us -> 92.2 us  [gradients(): pl.pallas_call(functools.partial(step_kernel, layers, seq_size), out_shap...]
    sub x7 -> x0, other arithmetic: 26 us -> none  [adam_update(): return (weight - rate * (ratio + DECAY * weight), new_first, new_second)]
    unnamed x53 -> x0, local copies, waits for them, and re-layouts: 17.6 us -> none
    reduce_sum x7 -> x0, other arithmetic: 15.8 us -> none  [local(): grad_norm = jnp.sqrt(sum((jnp.sum(grad * grad) for grad in averaged)))]
    transpose x3 -> x0, local copies, waits for them, and re-layouts: 4.39 us -> none  [the longest x2 3.55 us: unpack(): grads[at:at + ff].reshape(ff // 256, dims, 256).transpose(1, 0, 2)]
  transfers between devices with their start and end apart: 1 -> 0, of which waited for: 1 -> 0; matrix products, arithmetic and copies ran while one was open for 2% -> 0% of each run, Pallas kernels for 0% -> 0%
where the time goes in v2:
time: 181 us
  Pallas kernels  179 us (99%)
    pallas_call x1, Pallas kernels, gradients(): pl.pallas_call(functools.partial(step_kernel, layers, seq_size), out_shap...  92.2 us
    pallas_call x1, Pallas kernels, sum_gradients(): pl.pallas_call(functools.partial(sum_kernel, (seq_size, dp_size), buckets...  69.4 us
    pallas_call x1, Pallas kernels, update(): pl.pallas_call(functools.partial(update_kernel, layers), out_shape=tuple(...  17.4 us

profile of v2, /device:TPU:0, one launch (start us, length us, event | category | flops | bytes accessed | tf_op | source)
XLA Modules:
  0.0 181.0 jit_solution(490143848110048705)
XLA Ops:
  0.7 92.2 %train_step.1 = (bf16[2,7424,128]{2,1,0:T(8,128)(2,1)}, f32[8,128]{1,0:T(8,128)}) custom-call(s32[2,768]{1,0:T(2,128)} %codes_ref.1, s32[2,768]{1,0:T(2,128)} %actions_ref.1, s32[2,768]{1,0:T(2,128)} %next_ref.1, s32[2,8]{1,0:T(2,128)} %lengths_ref.1, f32[2,768]{1,0:T(2,128)} %rewards_ref.1, f32[2,768]{1,0:T(2,128)} %continues_ref.1, f32[2,768]{1,0:T(2,128)} %values_ref.1, ...), custom_call_target="tpu_custom_call" | custom-call | tf_op jit(solution)/shard_map/train_step/pallas_call | solution.py:600
  92.9 69.4 %sum_gradients.1 = (bf16[2,7424,128]{2,1,0:T(8,128)(2,1)}, f32[8,128]{1,0:T(8,128)}) custom-call(bf16[2,7424,128]{2,1,0:T(8,128)(2,1)} %get-tuple-element.49.source, f32[8,128]{1,0:T(8,128)} %get-tuple-element.50.scal_ref), custom_call_target="tpu_custom_call" | custom-call | tf_op jit(solution)/shard_map/sum_gradients/pallas_call | solution.py:960
  162.3 17.4 %update.1 = (f32[530,256]{1,0:T(8,128)}, f32[530,256]{1,0:T(8,128)}, f32[530,256]{1,0:T(8,128)}, f32[2,256,768]{2,1,0:T(8,128)}, f32[2,256,768]{2,1,0:T(8,128)},...) custom-call(f32[8,128]{1,0:T(8,128)} %get-tuple-element.51.scal_ref,, ...), custom_call_target="tpu_custom_call" | custom-call | tf_op jit(solution)/shard_map/update/pallas_call | solution.py:1104
  179.7 1.3 fusion

commit v3 on v2

--- a/solution.py
+++ b/solution.py
@@ -33,6 +33,18 @@
 OUTS = 544
 NEG = -1e30
 MESH = pl.DeviceIdType.MESH
+PER_ROW = 256 / 92e3
+TRANSFERS = {
+    "core": ("core", PER_ROW / 5.4, 1.1),
+    "one": ("seq", PER_ROW / 2, 2.8),
+    "two": ("seq", PER_ROW / 4, 2.8),
+    "all": ("seq", PER_ROW, 3.3),
+    "deep": ("deep", PER_ROW / 2, 3.5),
+    "tile": ("tile", 0.0, 3.6),
+}
+LONG = ("core", "one", "two", "deep", "back_deep", "back_two", "back_one", "back_core")
+SHORT = ("core", "all", "deep", "back_deep", "back_all", "back_core")
+STAGE_TIME = 0.35
 
 
 def dot_nn(left, right):
@@ -65,9 +77,371 @@
     return grad_x, jnp.sum((grad * unit).reshape(rows // 8, 8, dims), axis=0)
 
 
+def grad_row_count(layers):
+    rows = VOCAB + layers * 12 * 256 + OUTS + (OUTS - VOCAB) + 16
+    return -(-rows // 256) * 256
+
+
+def buckets_of(layers):
+    cuts = [0, VOCAB + 4 * 256]
+    for layer in range(layers):
+        cuts.append(cuts[-1] + 5 * 256)
+        cuts.append(cuts[-1] + (3 if layer == layers - 1 else 7) * 256)
+    cuts.append(grad_row_count(layers))
+    return list(zip(cuts[:-1], cuts[1:]))
+
+
+class Exchange:
+    def __init__(self, seq_size, dp_size, buckets, grads, out, core_in, one_in, two_in, two_out, deep_in,
+                 squares, tile_out, tile_in, send_sem, recv_sem, out_sem):
+        self.deep = dp_size // 2
+        self.owners = min(4, self.deep)
+        self.seq_size = seq_size
+        self.buckets = buckets
+        self.grads, self.out = grads, out
+        self.core_in, self.one_in, self.two_in, self.two_out = core_in, one_in, two_in, two_out
+        self.deep_in, self.squares = deep_in, squares
+        self.tile_out, self.tile_in = tile_out, tile_in
+        self.send_sem, self.recv_sem, self.out_sem = send_sem, recv_sem, out_sem
+        self.slots = exchange_slots(dp_size)
+        me = lax.axis_index("seq")
+        at_dp = lax.axis_index("dp")
+        self.me, self.core, self.at_deep = me, lax.rem(at_dp, 2), lax.div(at_dp, 2)
+        across = me + 1 - 2 * lax.rem(me, 2)
+        along = me + 2 - 4 * lax.div(me, 2)
+        self.first = across + self.core * (along - across)
+        self.second = along + self.core * (across - along)
+        self.opposite = 3 - me
+        self.sibling = {"dp": self.at_deep * 2 + 1 - self.core}
+        self.stage, self.due, self.free, self.now, self.summed = {}, {}, {}, 0.0, 0
+
+    def deep_peer(self, k):
+        return {"dp": lax.rem(self.at_deep + k, self.deep) * 2 + self.core}
+
+    def peers(self):
+        found = [self.sibling]
+        found += [{"seq": lax.rem(self.me + k, self.seq_size)} for k in range(1, self.seq_size)]
+        return found + [self.deep_peer(k) for k in range(1, self.deep)]
+
+    def greet(self):
+        for peer in self.peers():
+            pl.semaphore_signal(
+                pltpu.get_barrier_semaphore(), inc=1, device_id=peer, device_id_type=MESH
+            )
+
+    def greeted(self):
+        pl.semaphore_wait(pltpu.get_barrier_semaphore(), len(self.peers()))
+
+    def copy(self, src, dst, n, slot, peer):
+        return pltpu.make_async_remote_copy(
+            src_ref=src,
+            dst_ref=dst,
+            send_sem=self.send_sem.at[n, slot],
+            recv_sem=self.recv_sem.at[n, slot],
+            device_id=peer,
+            device_id_type=MESH,
+        )
+
+    def only(self, condition, act):
+        if self.owners == self.deep:
+            act()
+        else:
+            pl.when(condition)(act)
+
+    def parts(self, n):
+        r0, r1 = self.buckets[n]
+        quarter = (r1 - r0) // self.seq_size
+        return r0, r1 - r0, quarter, quarter // self.owners
+
+    def quarter_rows(self, n, index):
+        r0, _, quarter, _ = self.parts(n)
+        return pl.ds(pl.multiple_of(r0 + index * quarter, 16), quarter)
+
+    def packed_rows(self, n):
+        r0, _, quarter, _ = self.parts(n)
+        return pl.ds(r0 // self.seq_size, quarter)
+
+    def share_rows(self, n, index):
+        r0, _, _, share = self.parts(n)
+        return pl.ds(pl.multiple_of(r0 // self.seq_size + index * share, 16), share)
+
+    def own_rows(self, n):
+        r0, _, quarter, share = self.parts(n)
+        at = r0 + self.me * quarter + lax.rem(self.at_deep, self.owners) * share
+        return pl.ds(pl.multiple_of(at, 16), share)
+
+    def blocks(self, n, index, work):
+        r0, _, quarter, _ = self.parts(n)
+        size = quarter // 2 if quarter > 256 else quarter
+        for at in range(0, quarter, size):
+            wide = pl.ds(pl.multiple_of(r0 + index * quarter + at, 16), size)
+            work(wide, pl.ds(r0 // self.seq_size + at, size))
+
+    def core_copies(self, n):
+        r0, rows, _, _ = self.parts(n)
+        part = pl.ds(r0, rows)
+        return [self.copy(self.grads.at[1 - self.core, part], self.core_in.at[part], n, 0, self.sibling)]
+
+    def one_copies(self, n):
+        packed = self.packed_rows(n)
+        return [
+            self.copy(self.core_in.at[self.quarter_rows(n, q)], self.one_in.at[k, packed], n, 1 + k,
+                      {"seq": self.first})
+            for k, q in enumerate((self.first, self.opposite))
+        ]
+
+    def two_copies(self, n):
+        source = self.core_in.at[self.quarter_rows(n, self.second)]
+        return [self.copy(source, self.two_in.at[self.packed_rows(n)], n, 3, {"seq": self.second})]
+
+    def deep_copy(self, n, k):
+        r0, _, _, share = self.parts(n)
+        target = lax.rem(lax.rem(self.at_deep + k, self.deep), self.owners)
+        dest = self.deep_in.at[k - 1, pl.ds(r0 // (self.seq_size * self.owners), share)]
+        return self.copy(self.two_out.at[self.share_rows(n, target)], dest, n, 3 + k, self.deep_peer(k))
+
+    def back_copy(self, n, rows, slot, peer):
+        there = self.grads.at[self.core, rows]
+        return self.copy(there, there, n, self.slots // 2 + slot, peer)
+
+    def all_copies(self, n):
+        packed = self.packed_rows(n)
+        into = (self.one_in.at[0, packed], self.one_in.at[1, packed], self.two_in.at[packed])
+        found = []
+        for k in range(1, self.seq_size):
+            peer = lax.rem(self.me + k, self.seq_size)
+            source = self.core_in.at[self.quarter_rows(n, peer)]
+            found.append(self.copy(source, into[k - 1], n, k, {"seq": peer}))
+        return found
+
+    def back_all(self, n):
+        rows = self.quarter_rows(n, self.me)
+        return [
+            self.back_copy(n, rows, k, {"seq": lax.rem(self.me + k, self.seq_size)})
+            for k in range(1, self.seq_size)
+        ]
+
+    def back_two(self, n):
+        return [self.back_copy(n, self.quarter_rows(n, self.me), 3, {"seq": self.second})]
+
+    def back_one(self, n):
+        return [
+            self.back_copy(n, self.quarter_rows(n, q), 1 + k, {"seq": self.first})
+            for k, q in enumerate((self.me, self.second))
+        ]
+
+    def back_core(self, n):
+        r0, rows, _, _ = self.parts(n)
+        return [self.back_copy(n, pl.ds(r0, rows), 0, self.sibling)]
+
+    def out_copies(self, n):
+        r0, rows, _, _ = self.parts(n)
+        part = pl.ds(r0, rows)
+        return [
+            pltpu.make_async_copy(self.grads.at[side, part], self.out.at[side, part], self.out_sem.at[n, side])
+            for side in range(2)
+        ]
+
+    def start(self, copies):
+        for copy in copies:
+            copy.start()
+
+    def wait(self, copies):
+        for copy in copies:
+            copy.wait()
+
+    def add_in(self, n, quarters, more=()):
+        def work(wide, packed):
+            both = self.grads[self.core, wide, :].astype(F32) + self.core_in[wide, :].astype(F32)
+            for part in more:
+                both = both + part[packed, :].astype(F32)
+            self.core_in[wide, :] = both.astype(BF)
+
+        for q in quarters:
+            self.blocks(n, q, work)
+
+    def own_sum(self, n, wide, packed):
+        both = self.grads[self.core, wide, :].astype(F32) + self.core_in[wide, :].astype(F32)
+        both = both + self.one_in[0, packed, :].astype(F32)
+        if self.path(n) is SHORT:
+            both = both + self.one_in[1, packed, :].astype(F32)
+        return both + self.two_in[packed, :].astype(F32)
+
+    def after_core(self, n):
+        if self.path(n) is SHORT:
+            self.add_in(n, [lax.rem(self.me + k, self.seq_size) for k in range(1, self.seq_size)])
+        else:
+            self.add_in(n, (self.first, self.opposite))
+
+    def after_one(self, n):
+        self.add_in(n, (self.second,), (self.one_in.at[1],))
+
+    def after_two(self, n):
+        def work(wide, packed):
+            self.two_out[packed, :] = self.own_sum(n, wide, packed).astype(BF)
+
+        self.blocks(n, self.me, work)
+
+    def after_deep(self, n):
+        r0, _, _, share = self.parts(n)
+
+        def act():
+            rows = self.own_rows(n)
+            both = self.own_sum(n, rows, self.share_rows(n, lax.rem(self.at_deep, self.owners)))
+            part = pl.ds(r0 // (self.seq_size * self.owners), share)
+            for k in range(self.deep - 1):
+                both = both + self.deep_in[k, part, :].astype(F32)
+            self.grads[self.core, rows, :] = both.astype(BF)
+            self.squares[...] += jnp.sum((both * both).reshape(share // 8, 8, both.shape[1]), axis=0)
+
+        self.only(self.at_deep < self.owners, act)
+
+    def begin_deep(self, n):
+        for k in range(1, self.deep):
+            target = lax.rem(self.at_deep + k, self.deep)
+            self.only(target < self.owners, self.deep_copy(n, k).start)
+
+    def end_deep(self, n):
+        for k in range(1, self.deep):
+            target = lax.rem(self.at_deep + k, self.deep)
+            self.only(target < self.owners, self.deep_copy(n, k).wait_send)
+
+        def act():
+            for k in range(1, self.deep):
+                self.deep_copy(n, k).wait_recv()
+
+        self.only(self.at_deep < self.owners, act)
+
+    def begin_back_deep(self, n):
+        rows = self.own_rows(n)
+
+        def act():
+            for k in range(1, self.deep):
+                self.back_copy(n, rows, 3 + k, self.deep_peer(k)).start()
+
+        self.only(self.at_deep < self.owners, act)
+
+    def end_back_deep(self, n):
+        rows = self.own_rows(n)
+
+        def act():
+            for k in range(1, self.deep):
+                self.back_copy(n, rows, 3 + k, self.deep_peer(k)).wait_send()
+
+        self.only(self.at_deep < self.owners, act)
+        for k in range(1, self.deep):
+            origin = lax.rem(self.at_deep + self.deep - k, self.deep)
+            self.only(origin < self.owners, self.back_copy(n, rows, 3 + k, self.deep_peer(k)).wait_recv)
+
+    def path(self, n):
+        return SHORT if n >= len(self.buckets) - 2 else LONG
+
+    def begin_transfer(self, n, name):
+        if name == "deep":
+            self.begin_deep(n)
+        elif name == "back_deep":
+            self.begin_back_deep(n)
+        else:
+            self.start(getattr(self, name if "back" in name else name + "_copies")(n))
+
+    def end_transfer(self, n, name):
+        if name == "deep":
+            self.end_deep(n)
+        elif name == "back_deep":
+            self.end_back_deep(n)
+        else:
+            self.wait(getattr(self, name if "back" in name else name + "_copies")(n))
+        if name == "core":
+            self.after_core(n)
+        elif name == "one":
+            self.after_one(n)
+        elif name in ("two", "all"):
+            self.after_two(n)
+        elif name == "deep":
+            self.after_deep(n)
+        elif name == "back_core":
+            self.start(self.out_copies(n))
+
+    def launch(self, n):
+        step = self.stage[n]
+        if n < len(self.buckets):
+            name, rows = self.path(n)[step], self.buckets[n][1] - self.buckets[n][0]
+            self.begin_transfer(n, name)
+        else:
+            name, rows = "tile", 0
+            self.tile_start(n - len(self.buckets), step)
+        link, share, latency = TRANSFERS[name.replace("back_", "")]
+        self.free[link] = max(self.now, self.free.get(link, 0.0)) + rows * share
+        self.due[n] = self.free[link] + latency
+
+    def begin(self, n):
+        self.stage[n] = 0
+        self.launch(n)
+
+    def advance(self, n):
+        step = self.stage[n]
+        self.now = max(self.now, self.due.pop(n)) + STAGE_TIME
+        self.stage[n] += 1
+        if n < len(self.buckets):
+            path = self.path(n)
+            self.end_transfer(n, path[step])
+            self.summed += path[step] == "deep"
+            more = step + 1 < len(path)
+        else:
+            self.tile_finish(n - len(self.buckets), step)
+            more = step < 2
+        if more:
+            self.launch(n)
+        norm = len(self.buckets) + 1
+        if self.summed == len(self.buckets) and norm not in self.stage:
+            self.tile_out[1, 0] = self.squares[...]
+            self.begin(norm)
+
+    def tick(self, spent):
+        self.now += spent
+        for n in sorted(self.due):
+            if self.due[n] + 0.3 <= self.now:
+                self.advance(n)
+
+    def drain(self):
+        while self.due:
+            self.advance(min(self.due, key=lambda n: (self.due[n], n)))
+
+    def tile_copies(self, tile, phase):
+        if phase == 0:
+            slots, peers = [0], [self.sibling]
+        elif phase == 1:
+            slots = list(range(1, self.seq_size))
+            peers = [{"seq": lax.rem(self.me + k, self.seq_size)} for k in slots]
+        else:
+            slots = [3 + k for k in range(1, self.deep)]
+            peers = [self.deep_peer(k) for k in range(1, self.deep)]
+        n = len(self.buckets) + tile
+        return [
+            self.copy(self.tile_out.at[tile, phase], self.tile_in.at[tile, slot], n, slot, peer)
+            for slot, peer in zip(slots, peers)
+        ], slots
+
+    def tile_start(self, tile, phase):
+        self.start(self.tile_copies(tile, phase)[0])
+
+    def tile_finish(self, tile, phase):
+        copies, slots = self.tile_copies(tile, phase)
+        self.wait(copies)
+        both = self.tile_out[tile, phase]
+        for slot in slots:
+            both = both + self.tile_in[tile, slot]
+        self.tile_out[tile, phase + 1] = both
+
+
+def exchange_slots(dp_size):
+    return 2 * (4 + dp_size // 2 - 1)
+
+
 def step_kernel(
     layers,
-    seq_size,
+    sizes,
+    buckets,
     codes_ref,
     actions_ref,
     next_ref,
@@ -83,7 +457,7 @@
     ffn_out_ref,
     gains_ref,
     readout_ref,
-    grads_ref,
+    out_ref,
     scal_ref,
     wq,
     wo,
@@ -107,7 +481,7 @@
     gl,
     dmix,
     dqkv,
-    dkv,
+    carried,
     dgain,
     lossacc,
     lam,
@@ -116,6 +490,10 @@
     send_sem,
     recv_sem,
     load_sem,
+    table_f,
+    readout_f,
+    grads_ref,
+    *exchange_refs,
 ):
     batch, span = codes_ref.shape
     dims = gains_ref.shape[1]
@@ -133,14 +511,18 @@
     groups = HEADS // 2
     base = lax.axis_index("seq") * span
     me = lax.axis_index("seq")
+    seq_size = sizes[0]
     right = lax.rem(me + 1, seq_size)
     left = lax.rem(me + seq_size - 1, seq_size)
 
-    barrier = pltpu.get_barrier_semaphore()
-    for neighbour in (left, right):
-        pl.semaphore_signal(barrier, inc=1, device_id={"seq": neighbour}, device_id_type=MESH)
-    pl.semaphore_wait(barrier, 2)
-
+    ex = Exchange(*sizes, buckets, grads_ref, out_ref, *exchange_refs)
+    ex.greet()
+    ex.squares[...] = jnp.zeros_like(ex.squares)
+
+    loads = [
+        pltpu.make_async_copy(table_ref, table_f, load_sem.at[0]),
+        pltpu.make_async_copy(readout_ref, readout_f, load_sem.at[1]),
+    ]
     blocks = []
     for layer in range(layers):
         for j in range(3):
@@ -151,19 +533,27 @@
         for j in range(ff // 256):
             blocks.append((ffn_out_ref, wd, layer, slice(j * 256, j * 256 + 256), slice(0, 256)))
 
-    def block_copy(k):
-        source, _, layer, rows, cols = blocks[k]
-        at = 256 * (k % chunks)
-        return pltpu.make_async_copy(
-            source.at[layer, rows, cols], xs.at[1 + k // chunks, at : at + 256, :], load_sem.at[k]
+    def place_of(k):
+        at = (k + (2 * layers - 2) * chunks) % (2 * layers * chunks)
+        return 1 + at // chunks, slice(256 * (at % chunks), 256 * (at % chunks) + 256)
+
+    for k, (source, _, layer, rows, cols) in enumerate(blocks):
+        plane, there = place_of(k)
+        loads.append(
+            pltpu.make_async_copy(source.at[layer, rows, cols], xs.at[plane, there, :], load_sem.at[2 + k])
         )
-
-    for k in range(len(blocks)):
-        block_copy(k).start()
+    for load in loads:
+        load.start()
+
+    def convert(low, high):
+        for k in range(low, high):
+            _, dest, layer, rows, cols = blocks[k]
+            plane, there = place_of(k)
+            loads[2 + k].wait()
+            dest[layer, rows, cols] = xs[plane, there, :].astype(BF)
+
     tb[...] = jnp.zeros_like(tb)
-    tb[0:vocab_all, :] = table_ref[...].astype(BF)
     rt[...] = jnp.zeros_like(rt)
-    rt[0:outs_all, :] = readout_ref[...].astype(BF)
 
     ends = []
     for b in range(batch):
@@ -259,10 +649,8 @@
     def kv_rows(c):
         return pl.ds(pl.multiple_of(lax.rem(c, per_seq) * ROWS + SEG, 16), ROWS)
 
-    for k, (_, dest, layer, rows, cols) in enumerate(blocks):
-        block_copy(k).wait()
-        at = 256 * (k % chunks)
-        dest[layer, rows, cols] = xs[1 + k // chunks, at : at + 256, :].astype(BF)
+    loads[0].wait()
+    tb[0:vocab_all, :] = table_f[...].astype(BF)
 
     def onehot(c):
         code = toki[c, 0:1, :]
@@ -283,7 +671,7 @@
     odd_mask = jnp.where(lax.rem(lane_head, 2) == 1, 1.0, 0.0).astype(BF)
     even_f = lax.rem(lane_head, 2) == 0
 
-    def spread(rows):
+    def by_group(rows):
         return jnp.concatenate([rows * group_mask[g] for g in range(groups)], axis=0)
 
     def both(keys):
@@ -342,7 +730,7 @@
             keys = kvs[layer, b, window, 0:dims]
             values = kvs[layer, b, window, dims:]
             seen = causal & (key_place >= lows[b * pairs + pair, 0:1, :])
-            scores = dot_nt(both(keys), spread(qs[layer, rows, :]))
+            scores = dot_nt(both(keys), by_group(qs[layer, rows, :]))
             sides = []
             for side in range(2):
                 s = jnp.where(seen, scores[side * KEY : side * KEY + KEY], NEG)
@@ -387,10 +775,19 @@
 
         lax.fori_loop(0, chunks, body, 0)
 
+    per_layer = 4 + 2 * (ff // 256)
     for layer in range(layers):
+        if layer == 0:
+            convert(0, 3)
         project(layer)
+        if layer == 0:
+            ex.greeted()
         attend(layer)
+        if layer == 0:
+            convert(3, layers * per_layer)
         feed(layer)
+    loads[1].wait()
+    rt[0:outs_all, :] = readout_f[...].astype(BF)
 
     lossacc[...] = jnp.zeros_like(lossacc)
     dgain[...] = jnp.zeros_like(dgain)
@@ -451,6 +848,7 @@
         dh = dot_tn(gouts[:, rows], rt[...])
         grad_x, part = rms_pull(dh, x, top_gain)
         gx[rows, :] = grad_x
+        gl[rows, :] = grad_x.astype(BF)
         dgain[2 * layers] += part
         return carry
 
@@ -461,14 +859,19 @@
     loss_total = jnp.sum(lossacc[0:1, :])
     count_total = jnp.sum(lossacc[1:2, :])
     place = iota(scal_ref.shape, 0)
-    scal_ref[...] = jnp.where(place == 0, loss_total, jnp.where(place == 1, count_total, 0.0))
+    ex.tile_out[0, 0] = jnp.where(place == 0, loss_total, jnp.where(place == 1, count_total, 0.0))
+    ex.begin(len(buckets))
+
+    def spread(low, high, parts, spent, body):
+        for part in range(parts):
+            first = low + (high - low) * part // parts
+            lax.fori_loop(first, low + (high - low) * (part + 1) // parts, body, 0)
+            ex.tick(spent / parts)
 
     def feed_back(layer):
         def body(c, carry):
             rows = chunk_rows(c)
-            grad = gx[rows, :]
-            low = grad.astype(BF)
-            gl[rows, :] = low
+            low = gl[rows, :]
             for j in range(ff // 256):
                 cols = slice(j * 256, j * 256 + 256)
                 da = dot_nt(low, wd[layer, cols, :])
@@ -477,20 +880,22 @@
             gain = gains_ref[2 * layer + 1 : 2 * layer + 2, :]
             grad_x, part = rms_pull(dh, xs[2 * layer + 1, rows, :], gain)
             dgain[2 * layer + 1] += part
-            grad = grad + grad_x
+            grad = gx[rows, :] + grad_x
             gx[rows, :] = grad
-            dmix[rows, :] = dot_nt(grad.astype(BF), wo[layer]).astype(BF)
+            low = grad.astype(BF)
+            gl[rows, :] = low
+            dmix[rows, :] = dot_nt(low, wo[layer]).astype(BF)
             return carry
 
-        lax.fori_loop(0, chunks, body, 0)
+        spread(0, chunks, 3, 5.0, body)
 
     def attend_back(layer):
         def one(b, pair):
             rows, window = pair_rows(b, pair), pair_window(pair)
             keys = both(kvs[layer, b, window, 0:dims])
             values = both(kvs[layer, b, window, dims:])
-            queries = spread(qs[layer, rows, :])
-            dout = spread(dmix[rows, :])
+            queries = by_group(qs[layer, rows, :])
+            dout = by_group(dmix[rows, :])
             p = probs[layer, b * pairs + pair]
             dp = dot_nt(values, dout)
             sides = []
@@ -506,64 +911,76 @@
             dk = jnp.where(even_f, dk[0:KEY], dk[KEY:])
             dv = dot_nn(p, dout)
             dv = jnp.where(even_f, dv[0:KEY], dv[KEY:])
-            old = pl.ds(pl.multiple_of(pair * QRY, 16), SEG)
-            new = pl.ds(pl.multiple_of(pair * QRY + SEG, 16), QRY)
-            dkv[b, old, 0:dims] += dk[0:SEG]
-            dkv[b, old, dims:] += dv[0:SEG]
-            dkv[b, new, 0:dims] = dk[SEG:]
-            dkv[b, new, dims:] = dv[SEG:]
+            both_kv = jnp.concatenate([dk, dv], axis=1)
+            old = carried[b] + both_kv[0:SEG]
+            carried[b] = both_kv[QRY:]
+            here = pl.ds(pl.multiple_of(b * span + pair * QRY, 16), SEG)
+            dqkv[here, dims:] = both_kv[SEG:QRY].astype(BF)
+            return old.astype(BF)
 
         def body(pair, carry):
             for b in range(batch):
-                one(b, pair)
+                old = one(b, pair)
+                before = pl.ds(pl.multiple_of(b * span + pair * QRY - SEG, 16), SEG)
+                dqkv[before, dims:] = old
             return carry
 
+        carried[...] = jnp.zeros_like(carried)
         for b in range(batch):
-            dkv[b, 0:SEG, :] = jnp.zeros((SEG, 2 * dims), F32)
-        lax.fori_loop(0, 1, body, 0)
-        for b in range(batch):
-            bsend[layer, b] = dkv[b, 0:SEG, :].astype(BF)
+            bsend[layer, b] = one(b, 0)
         copy = backward_copy(layer)
         copy.start()
-        lax.fori_loop(1, pairs, body, 0)
+        ex.tick(1.1)
+        spread(1, pairs, 4, 7.6, body)
         copy.wait()
         for b in range(batch):
-            dkv[b, span : span + SEG, :] += brecv[layer, b].astype(F32)
+            final = carried[b] + brecv[layer, b].astype(F32)
+            dqkv[b * span + span - SEG : b * span + span, dims:] = final.astype(BF)
 
     def project_back(layer):
         def body(c, carry):
             rows = chunk_rows(c)
-            dqkv[rows, dims:] = dkv[c // per_seq, kv_rows(c), :].astype(BF)
             dh = dot_nt(dqkv[rows, :], wq[layer])
             gain = gains_ref[2 * layer : 2 * layer + 1, :]
             grad_x, part = rms_pull(dh, xs[2 * layer, rows, :], gain)
             dgain[2 * layer] += part
-            gx[rows, :] += grad_x
+            grad = gx[rows, :] + grad_x
+            gx[rows, :] = grad
+            gl[rows, :] = grad.astype(BF)
             return carry
 
-        lax.fori_loop(0, chunks, body, 0)
+        spread(0, chunks, 2, 2.1, body)
 
     at = VOCAB
+    bucket = 0
     for layer in reversed(range(layers)):
-        feed_back(layer)
         for j in range(ff // 256):
             cols = slice(j * 256, j * 256 + 256)
             put(at, dot_tn(acts[layer, :, cols], gl[...]))
             at += 256
+        ex.begin(bucket)
+        ex.tick(1.4)
+        feed_back(layer)
         for j in range(ff // 256):
             cols = slice(j * 256, j * 256 + 256)
             put(at, dot_tn(hs[2 * layer + 1], gds[layer, :, cols]))
             at += 256
-        gl[...] = gx[...].astype(BF)
+            if j % 2:
+                ex.tick(0.7)
         put(at, dot_tn(mixes[layer], gl[...]))
         at += 256
+        ex.begin(bucket + 1)
+        ex.tick(0.4)
         attend_back(layer)
-        project_back(layer)
         for j in range(3):
             cols = slice(j * 256, j * 256 + 256)
             put(at, dot_tn(hs[2 * layer], dqkv[:, cols]))
             at += 256
-    gl[...] = gx[...].astype(BF)
+        bucket += 2
+        if layer == 0:
+            ex.begin(bucket)
+        ex.tick(1.0)
+        project_back(layer)
 
     def mark(c, carry):
         gouts[:, chunk_rows(c)] = onehot(c)
@@ -571,6 +988,7 @@
 
     lax.fori_loop(0, chunks, mark, 0)
     put(at, dot_nn(gouts[...], gl[...]))
+    ex.tick(1.4)
     at = tail_at + OUTS - VOCAB
     place = iota((16, dims), 0)
     gain_rows = jnp.zeros((16, dims), F32)
@@ -579,9 +997,18 @@
     put(at, gain_rows)
     at += 16
     put(at, jnp.zeros((grads_ref.shape[1] - at, dims), F32))
-
-
-def gradients(codes, actions, next_codes, lengths, rewards, continues, values, weights, seq_size):
+    ex.begin(len(buckets) - 1)
+    ex.drain()
+    count = ex.tile_out[0, 3, 1:2, 0:1]
+    norm = jnp.sqrt(jnp.sum(ex.tile_out[1, 3]) / (count * count))
+    place = iota(scal_ref.shape, 0)
+    scal = jnp.where(place == 2, norm, ex.tile_out[0, 3])
+    scal_ref[...] = jnp.where(place == 3, jnp.minimum(1.0, CLIP_NORM / norm) / count, scal)
+    for n in range(len(buckets)):
+        ex.wait(ex.out_copies(n))
+
+
+def gradients(codes, actions, next_codes, lengths, rewards, continues, values, weights, sizes):
     table, attn_in, attn_out, ffn_in, ffn_out, gains, readout = weights
     batch, span = codes.shape
     layers, dims, ff = ffn_in.shape
@@ -589,6 +1016,11 @@
     tiles = span // SEG
     chunks = total // ROWS
     grad_rows = grad_row_count(layers)
+    buckets = buckets_of(layers)
+    seq_size, dp_size = sizes
+    owners = min(4, dp_size // 2)
+    slots = exchange_slots(dp_size)
+    hbm = pl.BlockSpec(memory_space=pltpu.HBM)
     steps = np.arange(lax.axis_size("seq") * tiles + 1, dtype=np.float64)[:, None]
     freq = np.exp(np.arange(dims // 2) * (-2.0 * math.log(10000.0) / dims))
     trig = np.zeros((steps.shape[0], 8, dims // 2), np.float32)
@@ -598,13 +1030,13 @@
     vmem = pl.BlockSpec(memory_space=pltpu.VMEM)
     smem = pl.BlockSpec(memory_space=pltpu.SMEM)
     return pl.pallas_call(
-        functools.partial(step_kernel, layers, seq_size),
+        functools.partial(step_kernel, layers, sizes, buckets),
         out_shape=(
             jax.ShapeDtypeStruct((2, grad_rows, dims // 2), BF),
             jax.ShapeDtypeStruct((8, 128), F32),
         ),
-        in_specs=[vmem] * 3 + [smem] + [vmem] * 5 + [pl.BlockSpec(memory_space=pltpu.HBM)] * 4 + [vmem] * 2,
-        out_specs=(vmem, vmem),
+        in_specs=[vmem] * 3 + [smem] + [vmem] * 4 + [hbm] * 5 + [vmem, hbm],
+        out_specs=(hbm, vmem),
         scratch_shapes=[
             pltpu.VMEM((layers, dims, 3 * dims), BF),
             pltpu.VMEM((layers, dims, dims), BF),
@@ -628,7 +1060,7 @@
             pltpu.VMEM((total, dims), BF),
             pltpu.VMEM((total, dims), BF),
             pltpu.VMEM((total, 3 * dims), BF),
-            pltpu.VMEM((batch, SEG + span, 2 * dims), F32),
+            pltpu.VMEM((batch, SEG, 2 * dims), F32),
             pltpu.VMEM((2 * layers + 1, 8, dims), F32),
             pltpu.VMEM((8, ROWS), F32),
             pltpu.VMEM((4, 8, span), F32),
@@ -636,7 +1068,21 @@
             pltpu.VMEM((layers, batch, SEG, 2 * dims), BF),
             pltpu.SemaphoreType.DMA((2 * layers,)),
             pltpu.SemaphoreType.DMA((2 * layers,)),
-            pltpu.SemaphoreType.DMA((12 * layers,)),
+            pltpu.SemaphoreType.DMA((2 + 12 * layers,)),
+            pltpu.VMEM(table.shape, F32),
+            pltpu.VMEM(readout.shape, F32),
+            pltpu.VMEM((2, grad_rows, dims // 2), BF),
+            pltpu.VMEM((grad_rows, dims // 2), BF),
+            pltpu.VMEM((2, grad_rows // seq_size, dims // 2), BF),
+            pltpu.VMEM((grad_rows // seq_size, dims // 2), BF),
+            pltpu.VMEM((grad_rows // seq_size, dims // 2), BF),
+            pltpu.VMEM((dp_size // 2 - 1, grad_rows // (seq_size * owners), dims // 2), BF),
+            pltpu.VMEM((8, dims // 2), F32),
+            pltpu.VMEM((2, 4, 8, 128), F32),
+            pltpu.VMEM((2, slots // 2, 8, 128), F32),
+            pltpu.SemaphoreType.DMA((len(buckets) + 2, slots)),
+            pltpu.SemaphoreType.DMA((len(buckets) + 2, slots)),
+            pltpu.SemaphoreType.DMA((len(buckets), 2)),
         ],
         compiler_params=pltpu.CompilerParams(
             collective_id=0, has_side_effects=True, vmem_limit_bytes=63 * 1024 * 1024
@@ -661,328 +1107,6 @@
     )
 
 
-def grad_row_count(layers):
-    rows = VOCAB + layers * 12 * 256 + OUTS + (OUTS - VOCAB) + 16
-    return -(-rows // 256) * 256
-
-
-def buckets_of(layers):
-    cuts = [0, VOCAB + 8 * 256]
-    for layer in range(layers):
-        cuts.append(cuts[-1] + 4 * 256)
-        if layer < layers - 1:
-            cuts.append(cuts[-1] + 8 * 256)
-    cuts[-1] = grad_row_count(layers)
-    return list(zip(cuts[:-1], cuts[1:]))
-
-
-class Exchange:
-    def __init__(self, seq_size, dp_size, source, total, core_in, seq_in, deep_in, sems):
-        self.seq_size, self.deep = seq_size, dp_size // 2
-        self.owners = min(4, self.deep)
-        self.source, self.total = source, total
-        self.core_in, self.seq_in, self.deep_in = core_in, seq_in, deep_in
-        self.send_sem, self.recv_sem = sems
-        self.at_seq = lax.axis_index("seq")
-        at_dp = lax.axis_index("dp")
-        self.core = lax.rem(at_dp, 2)
-        self.at_deep = lax.div(at_dp, 2)
-
-    def sibling(self):
-        return {"dp": self.at_deep * 2 + 1 - self.core}
-
-    def seq_peer(self, k):
-        return {"seq": lax.rem(self.at_seq + k, self.seq_size)}
-
-    def deep_peer(self, k):
-        return {"dp": lax.rem(self.at_deep + k, self.deep) * 2 + self.core}
-
-    def peers(self):
-        found = [self.sibling()]
-        found += [self.seq_peer(k) for k in range(1, self.seq_size)]
-        return found + [self.deep_peer(k) for k in range(1, self.deep)]
-
-    def greet(self):
-        barrier = pltpu.get_barrier_semaphore()
-        found = self.peers()
-        for peer in found:
-            pl.semaphore_signal(barrier, inc=1, device_id=peer, device_id_type=MESH)
-        pl.semaphore_wait(barrier, len(found))
-
-    def copy(self, src, dst, bucket, slot, peer):
-        return pltpu.make_async_remote_copy(
-            src_ref=src,
-            dst_ref=dst,
-            send_sem=self.send_sem.at[bucket, slot],
-            recv_sem=self.recv_sem.at[bucket, slot],
-            device_id=peer,
-            device_id_type=MESH,
-        )
-
-    def only(self, condition, act):
-        if self.owners == self.deep:
-            act()
-        else:
-            pl.when(condition)(act)
-
-    def slots(self):
-        return 2 * (1 + self.seq_size - 1 + self.deep - 1)
-
-    def parts(self, bucket):
-        r0, r1 = bucket
-        quarter = (r1 - r0) // self.seq_size
-        return r0, r1 - r0, quarter, quarter // self.owners
-
-    def seq_rows(self, bucket, index):
-        r0, _, quarter, _ = self.parts(bucket)
-        return pl.ds(pl.multiple_of(r0 + index * quarter, 16), quarter)
-
-    def share_rows(self, bucket, index):
-        r0, _, quarter, share = self.parts(bucket)
-        return pl.ds(pl.multiple_of(r0 // self.seq_size + index * share, 16), share)
-
-    def own_rows(self, bucket):
-        r0, _, quarter, share = self.parts(bucket)
-        at = r0 + self.at_seq * quarter + lax.rem(self.at_deep, self.owners) * share
-        return pl.ds(pl.multiple_of(at, 16), share)
-
-    def core_copy(self, n, bucket):
-        r0, rows, _, _ = self.parts(bucket)
-        part = pl.ds(r0, rows)
-        return self.copy(self.source.at[1 - self.core, part], self.core_in.at[part], n, 0, self.sibling())
-
-    def seq_copies(self, n, bucket):
-        r0, _, quarter, _ = self.parts(bucket)
-        found = []
-        for k in range(1, self.seq_size):
-            rows = self.seq_rows(bucket, lax.rem(self.at_seq + k, self.seq_size))
-            dest = self.seq_in.at[k - 1, pl.ds(r0 // self.seq_size, quarter)]
-            found.append(self.copy(self.core_in.at[rows], dest, n, k, self.seq_peer(k)))
-        return found
-
-    def deep_copy(self, n, bucket, k):
-        r0, _, _, share = self.parts(bucket)
-        target = lax.rem(self.at_deep + k, self.deep)
-        rows = self.share_rows(bucket, lax.rem(target, self.owners))
-        dest = self.deep_in.at[k - 1, pl.ds(r0 // (self.seq_size * self.owners), share)]
-        return self.copy(self.seq_out.at[rows], dest, n, self.seq_size - 1 + k, self.deep_peer(k))
-
-    def back_copy(self, n, rows, slot, peer):
-        there = self.total.at[self.core, rows]
-        return self.copy(there, there, n, self.slots() // 2 + slot, peer)
-
-    def core_start(self, n, bucket):
-        self.core_copy(n, bucket).start()
-
-    def core_finish(self, n, bucket):
-        self.core_copy(n, bucket).wait()
-        r0, rows, _, _ = self.parts(bucket)
-
-        def add(i, carry):
-            part = pl.ds(pl.multiple_of(r0 + i * 256, 256), 256)
-            both = self.source[self.core, part, :].astype(F32) + self.core_in[part, :].astype(F32)
-            self.core_in[part, :] = both.astype(BF)
-            return carry
-
-        lax.fori_loop(0, rows // 256, add, 0)
-
-    def seq_start(self, n, bucket):
-        for copy in self.seq_copies(n, bucket):
-            copy.start()
-
-    def seq_finish(self, n, bucket):
-        for copy in self.seq_copies(n, bucket):
-            copy.wait()
-        r0, _, quarter, _ = self.parts(bucket)
-
-        def add(i, carry):
-            here = pl.ds(pl.multiple_of(r0 + self.at_seq * quarter + i * 64, 16), 64)
-            part = pl.ds(pl.multiple_of(r0 // self.seq_size + i * 64, 16), 64)
-            both = self.core_in[here, :].astype(F32)
-            for k in range(self.seq_size - 1):
-                both = both + self.seq_in[k, part, :].astype(F32)
-            self.seq_out[part, :] = both.astype(BF)
-            return carry
-
-        lax.fori_loop(0, quarter // 64, add, 0)
-
-    def deep_start(self, n, bucket):
-        for k in range(1, self.deep):
-            target = lax.rem(self.at_deep + k, self.deep)
-            self.only(target < self.owners, self.deep_copy(n, bucket, k).start)
-
-    def deep_finish(self, n, bucket):
-        r0, _, _, share = self.parts(bucket)
-        for k in range(1, self.deep):
-            target = lax.rem(self.at_deep + k, self.deep)
-            self.only(target < self.owners, self.deep_copy(n, bucket, k).wait_send)
-
-        def act():
-            for k in range(1, self.deep):
-                self.deep_copy(n, bucket, k).wait_recv()
-            mine = self.share_rows(bucket, lax.rem(self.at_deep, self.owners))
-            both = self.seq_out[mine, :].astype(F32)
-            part = pl.ds(r0 // (self.seq_size * self.owners), share)
-            for k in range(self.deep - 1):
-                both = both + self.deep_in[k, part, :].astype(F32)
-            self.total[self.core, self.own_rows(bucket), :] = both.astype(BF)
-            squares = (both * both).reshape(share // 8, 8, both.shape[1])
-            self.squares[...] += jnp.sum(squares, axis=0)
-
-        self.only(self.at_deep < self.owners, act)
-
-    def back_deep(self, n, bucket, k):
-        return self.back_copy(n, self.own_rows(bucket), self.seq_size - 1 + k, self.deep_peer(k))
-
-    def back_deep_start(self, n, bucket):
-        def act():
-            for k in range(1, self.deep):
-                self.back_deep(n, bucket, k).start()
-
-        self.only(self.at_deep < self.owners, act)
-
-    def back_deep_finish(self, n, bucket):
-        def act():
-            for k in range(1, self.deep):
-                self.back_deep(n, bucket, k).wait_send()
-
-        self.only(self.at_deep < self.owners, act)
-        for k in range(1, self.deep):
-            origin = lax.rem(self.at_deep + self.deep - k, self.deep)
-            self.only(origin < self.owners, self.back_deep(n, bucket, k).wait_recv)
-
-    def back_seq(self, n, bucket):
-        rows = self.seq_rows(bucket, self.at_seq)
-        return [self.back_copy(n, rows, k, self.seq_peer(k)) for k in range(1, self.seq_size)]
-
-    def back_seq_start(self, n, bucket):
-        for copy in self.back_seq(n, bucket):
-            copy.start()
-
-    def back_seq_finish(self, n, bucket):
-        for copy in self.back_seq(n, bucket):
-            copy.wait()
-
-    def back_core(self, n, bucket):
-        r0, rows, _, _ = self.parts(bucket)
-        return self.back_copy(n, pl.ds(r0, rows), 0, self.sibling())
-
-    def back_core_start(self, n, bucket):
-        self.back_core(n, bucket).start()
-
-    def back_core_finish(self, n, bucket):
-        self.back_core(n, bucket).wait()
-
-    def tile_copies(self, n, tile, phase):
-        if phase == 0:
-            slots, peers = [0], [self.sibling()]
-        elif phase == 1:
-            slots = list(range(1, self.seq_size))
-            peers = [self.seq_peer(k) for k in slots]
-        else:
-            slots = [self.seq_size - 1 + k for k in range(1, self.deep)]
-            peers = [self.deep_peer(k) for k in range(1, self.deep)]
-        return [
-            self.copy(self.tile_out.at[tile, phase], self.tile_in.at[tile, slot], n, slot, peer)
-            for slot, peer in zip(slots, peers)
-        ], slots
-
-    def tile_start(self, n, tile, phase):
-        for copy in self.tile_copies(n, tile, phase)[0]:
-            copy.start()
-
-    def tile_finish(self, n, tile, phase):
-        copies, slots = self.tile_copies(n, tile, phase)
-        for copy in copies:
-            copy.wait()
-        both = self.tile_out[tile, phase]
-        for slot in slots:
-            both = both + self.tile_in[tile, slot]
-        self.tile_out[tile, phase + 1] = both
-
-
-def sum_kernel(sizes, buckets, source, scal_ref, total, out_ref, core_in, seq_in, seq_out, deep_in,
-               squares, tile_out, tile_in, send_sem, recv_sem):
-    ex = Exchange(*sizes, source, total, core_in, seq_in, deep_in, (send_sem, recv_sem))
-    ex.seq_out, ex.squares, ex.tile_out, ex.tile_in = seq_out, squares, tile_out, tile_in
-    ex.greet()
-    squares[...] = jnp.zeros_like(squares)
-    listed = list(enumerate(buckets))
-    first, second = len(buckets), len(buckets) + 1
-    tile_out[0, 0] = scal_ref[...]
-    for n, bucket in listed:
-        ex.core_start(n, bucket)
-    ex.tile_start(first, 0, 0)
-    for n, bucket in listed:
-        ex.core_finish(n, bucket)
-        ex.seq_start(n, bucket)
-    ex.tile_finish(first, 0, 0)
-    ex.tile_start(first, 0, 1)
-    for n, bucket in listed:
-        ex.seq_finish(n, bucket)
-        ex.deep_start(n, bucket)
-    ex.tile_finish(first, 0, 1)
-    ex.tile_start(first, 0, 2)
-    for n, bucket in listed:
-        ex.deep_finish(n, bucket)
-        ex.back_deep_start(n, bucket)
-    ex.tile_finish(first, 0, 2)
-    tile_out[1, 0] = squares[...]
-    ex.tile_start(second, 1, 0)
-    for n, bucket in listed:
-        ex.back_deep_finish(n, bucket)
-        ex.back_seq_start(n, bucket)
-    ex.tile_finish(second, 1, 0)
-    ex.tile_start(second, 1, 1)
-    for n, bucket in listed:
-        ex.back_seq_finish(n, bucket)
-        ex.back_core_start(n, bucket)
-    ex.tile_finish(second, 1, 1)
-    ex.tile_start(second, 1, 2)
-    ex.tile_finish(second, 1, 2)
-    for n, bucket in listed:
-        ex.back_core_finish(n, bucket)
-    count = tile_out[0, 3, 1:2, 0:1]
-    average = jnp.sum(tile_out[1, 3]) / (count * count)
-    norm = jnp.sqrt(average)
-    place = iota(out_ref.shape, 0)
-    out = jnp.where(place == 2, norm, tile_out[0, 3])
-    out_ref[...] = jnp.where(place == 3, jnp.minimum(1.0, CLIP_NORM / norm) / count, out)
-
-
-def sum_gradients(grads, scal, layers, seq_size, dp_size):
-    buckets = buckets_of(layers)
-    rows = grads.shape[1]
-    deep = dp_size // 2
-    owners = min(4, deep)
-    slots = 2 * (seq_size + deep - 1)
-    vmem = pl.BlockSpec(memory_space=pltpu.VMEM)
-    return pl.pallas_call(
-        functools.partial(sum_kernel, (seq_size, dp_size), buckets),
-        out_shape=(
-            jax.ShapeDtypeStruct(grads.shape, BF),
-            jax.ShapeDtypeStruct((8, 128), F32),
-        ),
-        in_specs=[vmem, vmem],
-        out_specs=(vmem, vmem),
-        scratch_shapes=[
-            pltpu.VMEM((rows, 128), BF),
-            pltpu.VMEM((seq_size - 1, rows // seq_size, 128), BF),
-            pltpu.VMEM((rows // seq_size, 128), BF),
-            pltpu.VMEM((deep - 1, rows // (seq_size * owners), 128), BF),
-            pltpu.VMEM((8, 128), F32),
-            pltpu.VMEM((2, 4, 8, 128), F32),
-            pltpu.VMEM((2, slots // 2, 8, 128), F32),
-            pltpu.SemaphoreType.DMA((len(buckets) + 2, slots)),
-            pltpu.SemaphoreType.DMA((len(buckets) + 2, slots)),
-        ],
-        compiler_params=pltpu.CompilerParams(
-            collective_id=1, has_side_effects=True, vmem_limit_bytes=62 * 1024 * 1024
-        ),
-        name="sum_gradients",
-    )(grads, scal)
-
-
 def adam_update(weight, first_mom, second_mom, clipped, rate):
     new_first = BETA_ONE * first_mom + (1.0 - BETA_ONE) * clipped
     new_second = BETA_TWO * second_mom + (1.0 - BETA_TWO) * clipped * clipped
@@ -994,9 +1118,9 @@
     return (weight - rate * (ratio + DECAY * weight), new_first, new_second)
 
 
-def update_kernel(layers, scal_ref, grads_ref, *refs):
+def update_kernel(layers, scal_ref, sums_ref, *refs):
     ins, outs, here = refs[0:21], refs[21:42], refs[42:63]
-    load_sem, store_sem = refs[63], refs[64]
+    load_sem, store_sem, sum_sem, grads_ref = refs[63:]
     scale = scal_ref[3, 0]
     pieces = [(slot, layer) for slot in (4, 3, 1, 2) for layer in range(layers)]
     pieces += [(0, None), (6, None), (5, None)]
@@ -1014,7 +1138,13 @@
             else:
                 yield pltpu.make_async_copy(inside, view(outs[index], layer), store_sem.at[n, part])
 
+    fetch = [
+        pltpu.make_async_copy(sums_ref.at[side], grads_ref.at[side], sum_sem.at[side]) for side in range(2)
+    ]
     for n in range(len(pieces)):
+        if n == 1:
+            for move in fetch:
+                move.start()
         for move in moves(n, 0):
             move.start()
 
@@ -1038,6 +1168,9 @@
     for n, (slot, layer) in enumerate(pieces):
         for move in moves(n, 0):
             move.wait()
+        if n == 0:
+            for move in fetch:
+                move.wait()
         if layer is not None:
             rows_all, cols_all = here[3 * slot].shape[1:]
             at = starts[slot, layer]
@@ -1106,12 +1239,17 @@
         out_shape=tuple(jax.ShapeDtypeStruct(x.shape, F32) for x in state),
         in_specs=[
             pl.BlockSpec(memory_space=pltpu.SMEM),
-            pl.BlockSpec(memory_space=pltpu.VMEM),
+            anywhere,
         ]
         + [anywhere] * 21,
         out_specs=(anywhere,) * 21,
         scratch_shapes=[pltpu.VMEM(x.shape, F32) for x in state]
-        + [pltpu.SemaphoreType.DMA((pieces, 3)), pltpu.SemaphoreType.DMA((pieces, 3))],
+        + [
+            pltpu.SemaphoreType.DMA((pieces, 3)),
+            pltpu.SemaphoreType.DMA((pieces, 3)),
+            pltpu.SemaphoreType.DMA((2,)),
+            pltpu.VMEM(grads.shape, BF),
+        ],
         compiler_params=pltpu.CompilerParams(vmem_limit_bytes=62 * 1024 * 1024),
         name="update",
     )(scal, grads, *state)
@@ -1121,11 +1259,10 @@
     state = state[0:18] + tuple(value.T for value in state[18:21])
     params = state[0::3]
     seq_size, dp_size = lax.axis_size("seq"), lax.axis_size("dp")
-    layers = params[1].shape[0]
+    sizes = (seq_size, dp_size)
     grads, scal = gradients(
-        codes, actions, next_codes, lengths, rewards, continues, target_values, params, seq_size
+        codes, actions, next_codes, lengths, rewards, continues, target_values, params, sizes
     )
-    grads, scal = sum_gradients(grads, scal, layers, seq_size, dp_size)
     results = list(update(grads, scal, state))
     results[18:21] = [value.T for value in results[18:21]]
     return tuple(results) + (scal[0, 0], scal[1, 0], scal[2, 0])

time: 181 us -> 145 us (0.80)
  Pallas kernels: 179 us -> 143 us
    pallas_call x2 -> x1, Pallas kernels: 162 us -> 123 us  [gradients(): pl.pallas_call(functools.partial(step_kernel, layers, sizes, buckets), ou...]
    pallas_call x1, Pallas kernels: 17.4 us -> 20.3 us  [update(): pl.pallas_call(functools.partial(update_kernel, layers), out_shape=tuple(...]
where the time goes in v3:
time: 145 us
  Pallas kernels  143 us (99%)
    pallas_call x1, Pallas kernels, gradients(): pl.pallas_call(functools.partial(step_kernel, layers, sizes, buckets), ou...  123 us
    pallas_call x1, Pallas kernels, update(): pl.pallas_call(functools.partial(update_kernel, layers), out_shape=tuple(...  20.3 us

profile of v3, /device:TPU:0, one launch (start us, length us, event | category | flops | bytes accessed | tf_op | source)
XLA Modules:
  0.0 145.1 jit_solution(16972380572256121374)
XLA Ops:
  0.7 122.9 %train_step.1 = (bf16[2,7424,128]{2,1,0:T(8,128)(2,1)}, f32[8,128]{1,0:T(8,128)}) custom-call(s32[2,768]{1,0:T(2,128)} %codes_ref.1, s32[2,768]{1,0:T(2,128)} %actions_ref.1, s32[2,768]{1,0:T(2,128)} %next_ref.1, s32[2,8]{1,0:T(2,128)} %lengths_ref.1, f32[2,768]{1,0:T(2,128)} %rewards_ref.1, f32[2,768]{1,0:T(2,128)} %continues_ref.1, f32[2,768]{1,0:T(2,128)} %values_ref.1, ...), custom_call_target="tpu_custom_call" | custom-call | tf_op jit(solution)/shard_map/train_step/pallas_call | solution.py:1032
  123.5 20.3 %update.1 = (f32[530,256]{1,0:T(8,128)}, f32[530,256]{1,0:T(8,128)}, f32[530,256]{1,0:T(8,128)}, f32[2,256,768]{2,1,0:T(8,128)}, f32[2,256,768]{2,1,0:T(8,128)},...) custom-call(f32[8,128]{1,0:T(8,128)} %get-tuple-element.47.scal_ref,, ...), custom_call_target="tpu_custom_call" | custom-call | tf_op jit(solution)/shard_map/update/pallas_call | solution.py:1237
  143.8 1.3 fusion
